TPU v7x, 256 devices: a whole 4x4x8 slice. The times are simulated.
256 devices in a mesh: batch: 16 (over z, core), tensor: 16 (over x, y).
Axes of the slice: x: 4, y: 4, z: 8, core: 2. Of those that a mesh axis runs over, the one named last changes fastest.
Arguments:
- tokens_qkv: bfloat16 [256, 2, 3, 4096], P('batch', None, None, 'tensor'), may hold values from -6 to 6
- residual_in: bfloat16 [256, 2, 8192], P('batch', None, 'tensor'), may hold values from -6 to 6
- state: float32 [256, 32, 128, 128], P('batch', 'tensor'), may hold values from -6 to 6
- decay_table: float32 [16], replicated, may hold values from 0.3 to 0.999
- decay_index: int32 [32], P('tensor'), may hold values from 0 to 15
- active: int32 [256], P('batch'), may hold values 0 or 1
- move_slot: int32 [16, 16], P('batch'), may hold values from 0 to 15, as said below
- move_dest: int32 [16, 16], P('batch'), may hold values from 0 to 15, as said below
- norm_gain: bfloat16 [8192], P('tensor'), may hold values from 0.5 to 1.5
- out_weight: bfloat16 [4096, 8192], P('tensor'), may hold values from -0.09375 to 0.09375
Outputs:
- normed: bfloat16 [256, 2, 8192], P('batch', None, 'tensor')
- residual_out: bfloat16 [256, 2, 8192], P('batch', None, 'tensor')
- new_state: float32 [256, 32, 128, 128], P('batch', 'tensor')
- arrived: float32 [512, 32, 128, 128], P('batch', 'tensor')
Inputs may be any that keep to these rules, and one draw needn't show every extreme that they name: `move_slot`: in each group's list the slots are distinct. `move_dest`: an entry naming its own group moves nothing; at most 2 entries of one list name one other group, and in every list some other group is named by exactly 2 entries.
All inputs are finite; a program needn't handle non-finite values. No bound on the sum of `active` on one device may be relied on, other than what follows from the above.
Results may differ from a plain program's by a relative error of at most 0.004.
Values may be sent and summed in bfloat16 or wider, within the bound.
No kernel may reach another device: no remote copies, remote signals or barrier semaphores. Data moves between devices by JAX's collectives and lax.ppermute only.
A program may use at most 64 MiB of HBM per device.

v0:
```python
import jax
import jax.numpy as jnp
from jax import lax
from jax.sharding import PartitionSpec as P

D = 8192
STEPS = 2
CAP = 2


def head_decays(decay_table, decay_index):
    table_ids = jnp.arange(decay_table.shape[0])
    picked = jnp.where(decay_index[:, None] == table_ids[None, :], decay_table[None, :], 0.0)
    return jnp.sum(picked, axis=1)


def advance(current, keys, values, flags, gamma):
    updated = gamma[None, :, None, None] * current + keys[..., :, None] * values[..., None, :]
    return jnp.where(flags[:, None, None, None], updated, current)


def readout(current, query, flags):
    raw = jnp.einsum("rhi,rhij->rhj", query, current, precision=lax.Precision.HIGHEST)
    scaled = raw * lax.rsqrt(jnp.mean(raw * raw, axis=-1, keepdims=True) + 1e-06)
    return jnp.where(flags[:, None, None], scaled, 0.0)


def body(
    tokens_qkv,
    residual_in,
    state,
    decay_table,
    decay_index,
    active,
    move_slot,
    move_dest,
    norm_gain,
    out_weight,
):
    count = state.shape[0]
    heads = state.shape[1]
    width = state.shape[2]
    groups = lax.axis_size("batch")
    group = lax.axis_index("batch")
    gamma = head_decays(decay_table, decay_index)
    flags = active > 0
    slots = move_slot[0]
    dests = move_dest[0]
    entries = slots.shape[0]
    moving = dests != group
    order = jnp.arange(entries)
    same = dests[:, None] == dests[None, :]
    ranks = jnp.sum(jnp.where(same & (order[None, :] < order[:, None]), 1, 0), axis=1).astype(
        jnp.int32
    )
    dest_ids = jnp.arange(groups)
    positions = jnp.arange(CAP)
    match = (
        moving[None, None, :]
        & (dests[None, None, :] == dest_ids[:, None, None])
        & (ranks[None, None, :] == positions[None, :, None])
    )
    chosen = jnp.sum(jnp.where(match, slots[None, None, :], 0), axis=2).reshape(groups * CAP)
    valid = jnp.any(match, axis=2).reshape(groups * CAP)
    slot_ids = jnp.arange(count)
    departed = jnp.any(moving[:, None] & (slots[:, None] == slot_ids[None, :]), axis=0)
    current = state
    outputs = []
    for step in range(STEPS):
        parts = tokens_qkv[:, step].astype(jnp.float32).reshape(count, 3, heads, width)
        current = advance(current, parts[:, 1], parts[:, 2], flags, gamma)
        outputs.append(readout(current, parts[:, 0], flags).reshape(count, heads * width))
    heads_out = (
        jnp.stack(outputs, axis=1).astype(jnp.bfloat16).reshape(count * STEPS, heads * width)
    )
    leaving = jnp.where(valid[:, None, None, None], jnp.take(current, chosen, axis=0), 0.0)
    arrived = lax.all_to_all(leaving, "batch", split_axis=0, concat_axis=0, tiled=True)
    new_state = jnp.where(departed[:, None, None, None], 0.0, current)
    partial_value = jnp.dot(heads_out, out_weight, preferred_element_type=jnp.float32).reshape(
        count, STEPS, D
    )
    share = residual_in.shape[2]
    gain = norm_gain.astype(jnp.float32)
    proj_full = lax.psum(partial_value, "tensor")
    residual_full = lax.all_gather(residual_in, "tensor", axis=2, tiled=True)
    hsum_full = residual_full.astype(jnp.float32) + proj_full
    mean_sq = jnp.mean(hsum_full * hsum_full, axis=-1, keepdims=True)
    hsum = lax.dynamic_slice_in_dim(hsum_full, lax.axis_index("tensor") * share, share, 2)
    normed = hsum * lax.rsqrt(mean_sq + 1e-05) * gain
    return (normed.astype(jnp.bfloat16), hsum.astype(jnp.bfloat16), new_state, arrived)


def solution(mesh):
    return jax.shard_map(
        body,
        mesh=mesh,
        in_specs=(
            P("batch", None, None, "tensor"),
            P("batch", None, "tensor"),
            P("batch", "tensor", None, None),
            P(),
            P("tensor"),
            P("batch"),
            P("batch", None),
            P("batch", None),
            P("tensor"),
            P("tensor", None),
        ),
        out_specs=(
            P("batch", None, "tensor"),
            P("batch", None, "tensor"),
            P("batch", "tensor", None, None),
            P("batch", "tensor", None, None),
        ),
        check_vma=False,
    )
```

profile of v0, /device:TPU:1, one launch (start us, length us, event | category | flops | bytes accessed | tf_op | source)
XLA Modules:
  0.0 155.5 jit_solution(11534662998250112577)
XLA Ops:
  7.2 0.7 broadcast_compare_fusion
  7.8 0.9 select_reduce_fusion
  8.8 0.8 fusion.16
  9.5 0.1 and_reduce_fusion
  9.6 0.8 fusion.7
  10.7 0.7 broadcast_compare_fusion.1
  11.3 0.1 copy.27
  11.4 0.1 broadcast_in_dim.126
  11.6 1.1 slice_reduce_fusion.1
  12.9 0.9 fusion.18
  13.7 3.5 %broadcast_select_fusion = (f32[16,2,128,128]{3,2,1,0:T(8,128)}, f32[16,2,128,128]{3,2,1,0:T(8,128)S(1)}) fusion(pred[16]{0:T(512)(128)(4,1)S(1)} %get-tuple-element.31, f32[16,2,128]{2,1,0:T(2,128)S(1)} %get-tuple-element.25, f32[16,2,128]{2,1,0:T(2,128)S(1)} %get-tuple-element.24, f32[16,2,128,128]{3,2,1,0:T(8,128)} %param.12, ...), kind=kLoop, calls=%fused_computation.7 | loop fusion | flops 4718592 | bytes 6357032 | tf_op jit(solution)/shard_map/jit(_where)/select_n | solution.py:78
  17.2 2.8 %gather_fusion = f32[32,2,128,128]{3,2,1,0:T(8,128)} fusion(f32[16,2,128,128]{3,2,1,0:T(8,128)S(1)} %get-tuple-element.19, s32[1024]{0:T(1024)S(1)} %pad_clamp_fusion), kind=kCustom, calls=%fused_computation | custom fusion | bytes 8388736 | tf_op jit(solution)/shard_map/jit(_take)/gather | solution.py:76
  20.0 5.2 %select_select_fusion = f32[32,2,128,128]{3,2,1,0:T(8,128)} fusion(f32[32,2,128,128]{3,2,1,0:T(8,128)} %gather_fusion, pred[32]{0:T(512)(128)(4,1)S(1)} %compare_and_fusion, pred[32]{0:T(512)(128)(4,1)S(1)} %broadcast_in_dim.126), kind=kLoop, calls=%fused_computation.3 | loop fusion | flops 2097152 | bytes 8388672 | tf_op jit(solution)/shard_map/jit(_where)/select_n | solution.py:76
  25.2 10.0 %all-to-all-start = ((f32[32,2,128,128]{3,2,1,0:T(8,128)}), f32[32,2,128,128]{3,2,1,0:T(8,128)}, u32[]{:S(2)}, u32[]{:S(2)}) async-start(f32[32,2,128,128]{3,2,1,0:T(8,128)} %select_select_fusion), calls=%async_computation | async-start | bytes 8388608 | tf_op jit(solution)/shard_map/all_to_all | solution.py:77
  35.2 3.0 %fusion.2 = f32[16,2,1,128]{3,2,1,0:T(1,128)S(1)} fusion(f32[16,2,128,128]{3,2,1,0:T(8,128)} %param.12, f32[16,2,128]{2,1,0:T(2,128)S(1)} %get-tuple-element.34, f32[16,2,128]{2,1,0:T(2,128)S(1)} %get-tuple-element.35, f32[2]{0:T(128)S(1)} %fusion.18, pred[16]{0:T(512)(128)(4,1)S(1)} %broadcast_compare_fusion.1, ...), kind=kOutput, calls=%fused_computation.6 | convolution fusion | flops 8388608 | bytes 2154520 | tf_op jit(solution)/shard_map/rhi,rhij->rhj/dot_general | solution.py:23
  38.3 1.1 fusion.11
  39.5 0.1 select_convert_fusion.1
  39.7 4.0 %fusion = f32[16,2,8192]{2,0,1:T(8,128)} fusion(bf16[256,8192]{1,0:T(8,128)(2,1)} %param.19, bf16[16,1,256]{2,0,1:T(8,128)(2,1)S(1)} %stack_reshape.9, bf16[16,1,256]{2,0,1:T(8,128)(2,1)S(1)} %stack_reshape.8), kind=kOutput, calls=%fused_computation.1 | convolution fusion | flops 134225920 | bytes 5259264 | tf_op jit(solution)/shard_map/dot_general | solution.py:79
  43.8 22.2 %all_gather.3 = bf16[16,2,8192]{2,0,1:T(8,128)(2,1)S(1)} all-gather(bf16[16,2,512]{2,0,1:T(8,128)(2,1)S(1)} %copy.24), channel_id=1, replica_groups=mesh['batch'=16,'tensor'=16] {'tensor'}, dimensions={2}, use_global_device_ids=true | all-gather | bytes 557056 | tf_op jit(solution)/shard_map/all_gather | solution.py:85
  66.0 75.1 %all-reduce.2.cloned.1.call-done = f32[16,2,8192]{2,0,1:T(8,128)} async-done(((f32[16,2,8192]{2,0,1:T(8,128)}), f32[16,2,8192]{2,0,1:T(8,128)}) %all-reduce.2.cloned.1.call-update) | async-done | bytes 1048592 | tf_op jit(solution)/shard_map/psum | solution.py:84
  141.1 1.5 multiply_reduce_fusion
  142.6 0.7 copy.31
  143.3 0.7 copy.30
  144.0 4.7 %copy.48 = f32[32,2,128,128]{3,2,1,0:T(8,128)} copy(f32[32,2,128,128]{3,2,1,0:T(8,128)} %all-to-all-done) | data formatting | bytes 8388608
  (32 shorter events, 0.8 us)
Async XLA Ops:
  25.2 118.8 %all-to-all-start = ((f32[32,2,128,128]{3,2,1,0:T(8,128)}), f32[32,2,128,128]{3,2,1,0:T(8,128)}, u32[]{:S(2)}, u32[]{:S(2)}) async-start(f32[32,2,128,128]{3,2,1,0:T(8,128)} %select_select_fusion), calls=%async_computation | async-start | bytes 8388608 | tf_op jit(solution)/shard_map/all_to_all | solution.py:77
  35.2 105.9 %all-reduce.2.cloned.1.call-start = ((), (), s32[]{:S(2)}) async-start(), calls=%async_computation.1 | async-start | bytes 2097152 | tf_op jit(solution)/shard_map/psum | solution.py:84
  39.7 4.1 %copy-start.1 = (bf16[512]{0:T(512)(128)(2,1)S(1)}, bf16[512]{0:T(512)(128)(2,1)}, u32[]{:S(2)}) copy-start(bf16[512]{0:T(512)(128)(2,1)} %param.18) | copy-start | bytes 3076
  39.7 4.1 %copy-start = (bf16[16,2,512]{2,1,0:T(2,128)(2,1)S(1)}, bf16[16,2,512]{2,1,0:T(2,128)(2,1)}, u32[]{:S(2)}) copy-start(bf16[16,2,512]{2,1,0:T(2,128)(2,1)} %param.11) | copy-start | bytes 98308
Sparse Core Ops, SparseCore 0:
  43.9 97.1 all-reduce.1
where the time goes:
time: 156 us
  waiting for transfers between devices  75.1 us (48%)
  blocking collectives  22.2 us (14%)
  other arithmetic  15.3 us (10%)
  between operations  14.2 us (9%)
  local copies, waits for them, and re-layouts  10.6 us (7%)
  starting transfers between devices  10 us (6%)
  matrix products  8.1 us (5%)
    psum x1, waiting for transfers between devices, body(): proj_full = lax.psum(partial_value, 'tensor')  75.1 us
    all_gather x1, blocking collectives, body(): residual_full = lax.all_gather(residual_in, 'tensor', axis=2, tiled=True)  22.2 us
    all_to_all x1, starting transfers between devices, body(): lax.all_to_all(leaving, 'batch', split_axis=0, concat_axis=0, tiled=True)  9.98 us
    unnamed x8, local copies, waits for them, and re-layouts  6.03 us
    select_n x1, other arithmetic, body(): jnp.where(valid[:, None, None, None], jnp.take(current, chosen, axis=0),...  5.15 us
    dot_general x2, matrix products, readout(): jnp.einsum('rhi,rhij->rhj', query, current, precision=lax.Precision.HIGHEST)  4.06 us
    dot_general x1, matrix products, body(): jnp.dot(heads_out, out_weight, preferred_element_type=jnp.float32)  4.04 us
    select_n x1, other arithmetic, body(): new_state = jnp.where(departed[:, None, None, None], 0.0, current)  3.49 us
  transfers between devices with their start and end apart: 2, of which 1 were waited for; matrix products, arithmetic and copies ran while one was open for 7% of the time, Pallas kernels for 0%

commit v1 on v0

v1 whole, which is shorter than its diff:
```python
import functools

import jax
import jax.numpy as jnp
from jax import lax
from jax.experimental import pallas as pl
from jax.experimental.pallas import tpu as pltpu
from jax.sharding import PartitionSpec as P

D = 8192
STEPS = 2
CAP = 2
SIDE = 4
W = 128

SMEM = pl.BlockSpec(memory_space=pltpu.SMEM)
VMEM = pl.BlockSpec(memory_space=pltpu.VMEM)


def decay(table_ref, index_ref, h):
    return table_ref[index_ref[h]]


def rows_of(k, v, gamma, h):
    kh = k[:, h * W : (h + 1) * W]
    vh = v[:, h * W : (h + 1) * W]
    row = lax.broadcasted_iota(jnp.int32, (8, W), 0)
    first = gamma * kh[0:1]
    hi = first.astype(jnp.bfloat16).astype(jnp.float32)
    mid = (first - hi).astype(jnp.bfloat16).astype(jnp.float32)
    low = first - hi - mid
    left = jnp.where(row == 0, hi, jnp.where(row == 1, mid, jnp.where(row == 2, low, jnp.where(row == 3, kh[1:2], 0.0))))
    right = jnp.where(row < 3, vh[0:1], jnp.where(row == 3, vh[1:2], 0.0))
    return left, right


def outer(left, right):
    return lax.dot_general(
        left.astype(jnp.bfloat16),
        right.astype(jnp.bfloat16),
        (((0,), (0,)), ((), ())),
        preferred_element_type=jnp.float32,
    )


def leave_kernel(table_ref, index_ref, active_ref, slot_ref, dest_ref, tok_ref, state_ref, out_ref, count_ref):
    me = lax.axis_index("batch")
    entries = slot_ref.shape[1]
    heads = state_ref.shape[1]
    for g in range(count_ref.shape[0]):
        count_ref[g] = 0
    out_ref[...] = jnp.zeros_like(out_ref)

    def entry(j, carry):
        slot = slot_ref[0, j]
        dest = dest_ref[0, j]
        position = count_ref[dest]
        count_ref[dest] = position + 1

        @pl.when((dest != me) & (position < CAP))
        def _():
            on = active_ref[slot] > 0
            tokens = tok_ref[slot].astype(jnp.float32)
            for h in range(heads):
                gamma = decay(table_ref, index_ref, h)
                left, right = rows_of(tokens[1], tokens[2], gamma, h)
                left = jnp.where(on, left, 0.0)
                keep = jnp.where(on, gamma * gamma, 1.0)
                final = keep * state_ref[slot, h] + outer(left, right)
                out_ref[dest * CAP + position, h] = final.astype(jnp.bfloat16)

        return carry

    lax.fori_loop(0, entries, entry, 0)


def decode_kernel(
    table_ref, index_ref, active_ref, slot_ref, dest_ref, tok_ref, state_ref, new_ref, heads_ref, gone_ref
):
    me = lax.axis_index("batch")
    entries = slot_ref.shape[1]
    heads = state_ref.shape[1]
    i = pl.program_id(0)

    @pl.when(i == 0)
    def _():
        for s in range(gone_ref.shape[0]):
            gone_ref[s] = 0
        for j in range(entries):
            slot = slot_ref[0, j]
            moves = jnp.where(dest_ref[0, j] != me, 1, 0)
            gone_ref[slot] = gone_ref[slot] + moves

    on = active_ref[i] > 0
    gone = gone_ref[i] > 0
    tokens = tok_ref[0].astype(jnp.float32)
    query, key, value = tokens[0], tokens[1], tokens[2]
    row = lax.broadcasted_iota(jnp.int32, (8, W), 0)
    wide = lax.broadcasted_iota(jnp.int32, (8, 2 * W), 0)
    lane = lax.broadcasted_iota(jnp.int32, (8, 2 * W), 1)
    ones = jnp.where((wide == 4) & (lane < W), 1.0, jnp.where((wide == 5) & (lane >= W), 1.0, 0.0))
    for h in range(heads):
        part = slice(h * W, (h + 1) * W)
        q, k, v = query[:, part], key[:, part], value[:, part]
        gamma = decay(table_ref, index_ref, h)
        left, right = rows_of(key, value, gamma, h)
        left = jnp.where(row == 4, q[0:1], jnp.where(row == 5, q[1:2], left))
        mixed = outer(left, jnp.concatenate([right, ones], axis=1))
        before = state_ref[0, h]
        raw1 = gamma * jnp.sum(mixed[:, W : 2 * W] * before, axis=0, keepdims=True)
        raw1 = raw1 + jnp.sum(q[0:1] * k[0:1], axis=1, keepdims=True) * v[0:1]
        final = (gamma * gamma) * before + mixed[:, :W]
        raw2 = jnp.sum(mixed[:, 2 * W :] * final, axis=0, keepdims=True)
        raw = jnp.where(row == 0, raw1, jnp.where(row == 1, raw2, 0.0))
        scaled = raw * lax.rsqrt(jnp.mean(raw * raw, axis=1, keepdims=True) + 1e-06)
        heads_ref[0, :, part] = jnp.where(on, scaled, 0.0)
        final = jnp.where(on, final, before)
        new_ref[0, h] = jnp.where(gone, 0.0, final)


def project_kernel(heads_ref, weight_ref, *out_refs):
    me = lax.axis_index("tensor")
    x = me // SIDE
    y = me % SIDE
    share = weight_ref.shape[1] // (SIDE * SIDE)
    count, padded, depth = heads_ref.shape
    rows = count * STEPS
    row = lax.broadcasted_iota(jnp.int32, (rows, count * padded), 0)
    source = lax.broadcasted_iota(jnp.int32, (rows, count * padded), 1)
    pick = jnp.where(source == (row // STEPS) * padded + row % STEPS, 1.0, 0.0).astype(jnp.bfloat16)
    heads = heads_ref[...].reshape(count * padded, depth).astype(jnp.bfloat16)
    heads = jnp.dot(pick, heads, preferred_element_type=jnp.float32).astype(jnp.bfloat16)
    for dx in range(SIDE):
        for dy in range(SIDE):
            block = ((x + dx) % SIDE) * SIDE + (y + dy) % SIDE
            columns = pl.ds(pl.multiple_of(block * share, share), share)
            out_refs[dx][dy] = jnp.dot(heads, weight_ref[:, columns], preferred_element_type=jnp.float32)


def add_kernel(a_ref, b_ref, c_ref, d_ref, *out_refs):
    for dy in range(SIDE):
        out_refs[dy][...] = (a_ref[dy] + b_ref[dy]) + (c_ref[dy] + d_ref[dy])


def residual_kernel(residual_ref, a_ref, b_ref, c_ref, d_ref, hsum_ref, square_ref):
    hsum = residual_ref[...].astype(jnp.float32) + ((a_ref[...] + b_ref[...]) + (c_ref[...] + d_ref[...]))
    hsum_ref[...] = hsum
    square_ref[...] = jnp.broadcast_to(jnp.sum(hsum * hsum, axis=1, keepdims=True), square_ref.shape)


def shift_x(value, d):
    return lax.ppermute(
        value, "tensor", [(x * SIDE + y, ((x + d) % SIDE) * SIDE + y) for x in range(SIDE) for y in range(SIDE)]
    )


def shift_y(value, d):
    return lax.ppermute(
        value, "tensor", [(x * SIDE + y, x * SIDE + (y + d) % SIDE) for x in range(SIDE) for y in range(SIDE)]
    )


def body(
    tokens_qkv,
    residual_in,
    state,
    decay_table,
    decay_index,
    active,
    move_slot,
    move_dest,
    norm_gain,
    out_weight,
):
    count, heads, width, _ = state.shape
    groups = lax.axis_size("batch")
    rows = count * STEPS
    share = residual_in.shape[2]
    f32 = jnp.float32
    tokens = jnp.transpose(tokens_qkv, (0, 2, 1, 3))
    scalars = (decay_table, decay_index, active, move_slot, move_dest)

    leaving = pl.pallas_call(
        leave_kernel,
        out_shape=jax.ShapeDtypeStruct((groups * CAP, heads, width, width), jnp.bfloat16),
        in_specs=[SMEM] * 5 + [VMEM] * 2,
        out_specs=VMEM,
        scratch_shapes=[pltpu.SMEM((groups,), jnp.int32)],
        compiler_params=pltpu.CompilerParams(vmem_limit_bytes=24 << 20),
        cost_estimate=pl.CostEstimate(flops=32 * 10 * width * width, bytes_accessed=4 << 20, transcendentals=0),
        name="leave",
    )(*scalars, tokens, state)
    landed = lax.all_to_all(leaving, "batch", split_axis=0, concat_axis=0, tiled=True)

    new_state, heads_out = pl.pallas_call(
        decode_kernel,
        grid=(count,),
        out_shape=(
            jax.ShapeDtypeStruct(state.shape, f32),
            jax.ShapeDtypeStruct((count, 8, heads * width), f32),
        ),
        in_specs=[SMEM] * 5
        + [
            pl.BlockSpec((1, 3, STEPS, heads * width), lambda i: (i, 0, 0, 0)),
            pl.BlockSpec((1, heads, width, width), lambda i: (i, 0, 0, 0)),
        ],
        out_specs=(
            pl.BlockSpec((1, heads, width, width), lambda i: (i, 0, 0, 0)),
            pl.BlockSpec((1, 8, heads * width), lambda i: (i, 0, 0)),
        ),
        scratch_shapes=[pltpu.SMEM((count,), jnp.int32)],
        compiler_params=pltpu.CompilerParams(vmem_limit_bytes=24 << 20),
        cost_estimate=pl.CostEstimate(flops=32 * 20 * width * width, bytes_accessed=4 << 20, transcendentals=0),
        name="decode",
    )(*scalars, tokens, state)

    parts = pl.pallas_call(
        project_kernel,
        out_shape=[jax.ShapeDtypeStruct((SIDE, rows, share), f32)] * SIDE,
        in_specs=[VMEM] * 2,
        out_specs=[VMEM] * SIDE,
        compiler_params=pltpu.CompilerParams(vmem_limit_bytes=24 << 20),
        cost_estimate=pl.CostEstimate(flops=2 * rows * heads * width * D, bytes_accessed=5 << 20, transcendentals=0),
        name="project",
    )(heads_out, out_weight)
    lines = [parts[0]] + [shift_x(parts[d], d) for d in range(1, SIDE)]
    sums = pl.pallas_call(
        add_kernel,
        out_shape=[jax.ShapeDtypeStruct((rows, share), f32)] * SIDE,
        in_specs=[VMEM] * SIDE,
        out_specs=[VMEM] * SIDE,
        name="add",
    )(*lines)
    terms = [sums[0]] + [shift_y(sums[d], d) for d in range(1, SIDE)]
    residual = residual_in.reshape(rows, share)
    hsum, square = pl.pallas_call(
        residual_kernel,
        out_shape=(jax.ShapeDtypeStruct((rows, share), f32), jax.ShapeDtypeStruct((rows, W), f32)),
        in_specs=[VMEM] * 5,
        out_specs=(VMEM, VMEM),
        name="residual",
    )(residual, *terms)
    square = square + (shift_x(square, 1) + shift_x(square, 2) + shift_x(square, 3))
    square = square + (shift_y(square, 1) + shift_y(square, 2) + shift_y(square, 3))
    normed = hsum * lax.rsqrt(square[:, :1] / D + 1e-05) * norm_gain.astype(f32)

    def place(value):
        return value.astype(jnp.bfloat16).reshape(count, STEPS, share)

    return (place(normed), place(hsum), new_state, landed.astype(f32))


def solution(mesh):
    return jax.shard_map(
        body,
        mesh=mesh,
        in_specs=(
            P("batch", None, None, "tensor"),
            P("batch", None, "tensor"),
            P("batch", "tensor", None, None),
            P(),
            P("tensor"),
            P("batch"),
            P("batch", None),
            P("batch", None),
            P("tensor"),
            P("tensor", None),
        ),
        out_specs=(
            P("batch", None, "tensor"),
            P("batch", None, "tensor"),
            P("batch", "tensor", None, None),
            P("batch", "tensor", None, None),
        ),
        check_vma=False,
    )
```

time: 156 us -> 86.5 us (0.55)
  the two profiles are of different devices: /device:TPU:1 before, /device:TPU:32 now
where the time goes in v1:
time: 86.5 us; the launch traced here: 85.8 us
  starting transfers between devices  27.8 us (32%)
  waiting for transfers between devices  21.8 us (25%)
  Pallas kernels  16.2 us (19%)
  local copies, waits for them, and re-layouts  13.2 us (15%)
  other arithmetic  5.97 us (7%)
    ppermute x6, waiting for transfers between devices, shift_x(): lax.ppermute(value, 'tensor', [(x * SIDE + y, (x + d) % SIDE * SIDE + y)...  15 us
    unnamed x50, local copies, waits for them, and re-layouts  11.3 us
    ppermute x6, starting transfers between devices, shift_x(): lax.ppermute(value, 'tensor', [(x * SIDE + y, (x + d) % SIDE * SIDE + y)...  9.63 us
    ppermute x6, starting transfers between devices, shift_y(): lax.ppermute(value, 'tensor', [(x * SIDE + y, x * SIDE + (y + d) % SIDE)...  9.33 us
    all_to_all x1, starting transfers between devices, body(): lax.all_to_all(leaving, 'batch', split_axis=0, concat_axis=0, tiled=True)  8.82 us
    pallas_call x1, Pallas kernels, body(): pl.pallas_call(decode_kernel, grid=(count,), out_shape=(jax.ShapeDtypeStr...  8.47 us
    ppermute x6, waiting for transfers between devices, shift_y(): lax.ppermute(value, 'tensor', [(x * SIDE + y, x * SIDE + (y + d) % SIDE)...  6.78 us
    convert_element_type x1, other arithmetic, body(): return (place(normed), place(hsum), new_state, landed.astype(f32))  4.13 us
  transfers between devices with their start and end apart: 13, of which 8 were waited for; matrix products, arithmetic and copies ran while one was open for 4% of the time, Pallas kernels for 15%

profile of v1, /device:TPU:32, one launch (start us, length us, event | category | flops | bytes accessed | tf_op | source)
XLA Modules:
  0.0 85.8 jit_solution(308634596044306057)
XLA Ops:
  0.6 1.6 %copy-done = f32[16,2,128,128]{3,2,1,0:T(8,128)S(1)} copy-done((f32[16,2,128,128]{3,2,1,0:T(8,128)S(1)}, f32[16,2,128,128]{3,2,1,0:T(8,128)}, u32[]{:S(2)}) %copy-start) | copy-done | bytes 2097176
  6.3 3.3 %leave.1 = bf16[32,2,128,128]{3,2,1,0:T(8,128)(2,1)S(1)} custom-call(f32[16]{0:T(128)S(1)} %copy-done.7, s32[2]{0:T(128)S(1)} %copy-done.9, s32[16]{0:T(128)S(1)} %copy-done.11, s32[1,16]{1,0:T(1,128)S(1)} %copy-done.13, s32[1,16]{1,0:T(1,128)S(1)} %copy-done.15, bf16[16,3,2,256]{3,2,1,0:T(2,128)(2,1)S(1)} %bitcast.1, f32[16,2,128,128]{3,2,1,0:T(8,128)S(1)} %copy-done), custom_call_target="tpu_custom_call" | custom-call | flops 5242880 | bytes 4194304 | tf_op jit(solution)/shard_map/leave/pallas_call | solution.py:183
  9.6 1.3 %copy-done.2 = bf16[32,2,128,128]{3,2,1,0:T(8,128)(2,1)} copy-done((bf16[32,2,128,128]{3,2,1,0:T(8,128)(2,1)}, bf16[32,2,128,128]{3,2,1,0:T(8,128)(2,1)S(1)}, u32[]{:S(2)}) %copy-start.2) | copy-done | bytes 2097176
  11.0 8.8 %all-to-all-start = ((bf16[32,2,128,128]{3,2,1,0:T(8,128)(2,1)}), bf16[32,2,128,128]{3,2,1,0:T(8,128)(2,1)}, u32[]{:S(2)}, u32[]{:S(2)}) async-start(bf16[32,2,128,128]{3,2,1,0:T(8,128)(2,1)} %copy-done.2), calls=%async_computation | async-start | bytes 4194304 | tf_op jit(solution)/shard_map/all_to_all | solution.py:193
  19.8 8.5 %decode.1 = (f32[16,2,128,128]{3,2,1,0:T(8,128)}, f32[16,8,256]{2,1,0:T(8,128)S(1)}) custom-call(f32[16]{0:T(128)S(1)} %copy-done.8, s32[2]{0:T(128)S(1)} %copy-done.10, s32[16]{0:T(128)S(1)} %copy-done.12, s32[1,16]{1,0:T(1,128)S(1)} %copy-done.14, s32[1,16]{1,0:T(1,128)S(1)} %copy-done.16, bf16[16,3,2,256]{3,2,1,0:T(2,128)(2,1)S(1)} %bitcast.2, ...), custom_call_target="tpu_custom_call" | custom-call | flops 10485760 | bytes 4194304 | tf_op jit(solution)/shard_map/decode/pallas_call | solution.py:195
  28.3 2.2 %copy-done.3 = bf16[256,8192]{1,0:T(8,128)(2,1)S(1)} copy-done((bf16[256,8192]{1,0:T(8,128)(2,1)S(1)}, bf16[256,8192]{1,0:T(8,128)(2,1)}, u32[]{:S(2)}) %copy-start.3) | copy-done | bytes 4194328
  32.2 1.5 %collective-permute-start = (f32[4,32,512]{2,1,0:T(8,128)S(1)}, f32[4,32,512]{2,1,0:T(8,128)S(1)}, u32[]{:S(2)}, u32[]{:S(2)}) collective-permute-start(f32[4,32,512]{2,1,0:T(8,128)S(1)} %get-tuple-element.18), channel_id=1, source_target_pairs={{0,4},{1,5},{2,6},{3,7},{4,8},{5,9},{6,10},{7,11},{8,12},{9,13},{1... | collective-permute-start | bytes 786440 | tf_op jit(solution)/shard_map/ppermute | solution.py:152
  33.7 2.7 %collective-permute-start.1 = (f32[4,32,512]{2,1,0:T(8,128)S(1)}, f32[4,32,512]{2,1,0:T(8,128)S(1)}, u32[]{:S(2)}, u32[]{:S(2)}) collective-permute-start(f32[4,32,512]{2,1,0:T(8,128)S(1)} %get-tuple-element.19), channel_id=1, source_target_pairs={{0,8},{1,9},{2,10},{3,11},{4,12},{5,13},{6,14},{7,15},{8,0},{9,1},... | collective-permute-start | bytes 786440 | tf_op jit(solution)/shard_map/ppermute | solution.py:152
  36.4 1.4 %collective-permute-start.2 = (f32[4,32,512]{2,1,0:T(8,128)S(1)}, f32[4,32,512]{2,1,0:T(8,128)S(1)}, u32[]{:S(2)}, u32[]{:S(2)}) collective-permute-start(f32[4,32,512]{2,1,0:T(8,128)S(1)} %get-tuple-element.20), channel_id=1, source_target_pairs={{0,12},{1,13},{2,14},{3,15},{4,0},{5,1},{6,2},{7,3},{8,4},{9,5},{1... | collective-permute-start | bytes 786440 | tf_op jit(solution)/shard_map/ppermute | solution.py:152
  37.8 3.9 %collective-permute-done.b_ref = f32[4,32,512]{2,1,0:T(8,128)S(1)} collective-permute-done((f32[4,32,512]{2,1,0:T(8,128)S(1)}, f32[4,32,512]{2,1,0:T(8,128)S(1)}, u32[]{:S(2)}, u32[]{:S(2)}) %collective-permute-start) | collective-permute-done | bytes 262176 | tf_op jit(solution)/shard_map/ppermute | solution.py:152
  41.7 6.6 %collective-permute-done.1.c_ref = f32[4,32,512]{2,1,0:T(8,128)S(1)} collective-permute-done((f32[4,32,512]{2,1,0:T(8,128)S(1)}, f32[4,32,512]{2,1,0:T(8,128)S(1)}, u32[]{:S(2)}, u32[]{:S(2)}) %collective-permute-start.1) | collective-permute-done | bytes 262176 | tf_op jit(solution)/shard_map/ppermute | solution.py:152
  49.1 1.9 %add.58 = (f32[32,512]{1,0:T(8,128)}, f32[32,512]{1,0:T(8,128)}, f32[32,512]{1,0:T(8,128)}, f32[32,512]{1,0:T(8,128)}) custom-call(f32[4,32,512]{2,1,0:T(8,128)} %copy-done.4, f32[4,32,512]{2,1,0:T(8,128)} %copy-done.17, f32[4,32,512]{2,1,0:T(8,128)} %copy-done.18, f32[4,32,512]{2,1,0:T(8,128)} %copy-done.19), custom_call_target="tpu_custom_call" | custom-call | tf_op jit(solution)/shard_map/add/pallas_call | solution.py:227
  51.0 1.6 %collective-permute-start.3 = (f32[32,512]{1,0:T(8,128)}, f32[32,512]{1,0:T(8,128)S(1)}, u32[]{:S(2)}, u32[]{:S(2)}) collective-permute-start(f32[32,512]{1,0:T(8,128)} %get-tuple-element.22), channel_id=1, source_target_pairs={{0,1},{1,2},{2,3},{3,0},{4,5},{5,6},{6,7},{7,4},{8,9},{9,10},{10,1... | collective-permute-start | bytes 196616 | tf_op jit(solution)/shard_map/ppermute | solution.py:158
  52.6 2.9 %collective-permute-start.4 = (f32[32,512]{1,0:T(8,128)}, f32[32,512]{1,0:T(8,128)S(1)}, u32[]{:S(2)}, u32[]{:S(2)}) collective-permute-start(f32[32,512]{1,0:T(8,128)} %get-tuple-element.23), channel_id=1, source_target_pairs={{0,2},{1,3},{2,0},{3,1},{4,6},{5,7},{6,4},{7,5},{8,10},{9,11},{10,... | collective-permute-start | bytes 196616 | tf_op jit(solution)/shard_map/ppermute | solution.py:158
  55.5 1.3 %collective-permute-start.5 = (f32[32,512]{1,0:T(8,128)}, f32[32,512]{1,0:T(8,128)S(1)}, u32[]{:S(2)}, u32[]{:S(2)}) collective-permute-start(f32[32,512]{1,0:T(8,128)} %get-tuple-element.24), channel_id=1, source_target_pairs={{0,3},{1,0},{2,1},{3,2},{4,7},{5,4},{6,5},{7,6},{8,11},{9,8},{10,9... | collective-permute-start | bytes 196616 | tf_op jit(solution)/shard_map/ppermute | solution.py:158
  57.5 1.2 %collective-permute-done.4.c_ref = f32[32,512]{1,0:T(8,128)S(1)} collective-permute-done((f32[32,512]{1,0:T(8,128)}, f32[32,512]{1,0:T(8,128)S(1)}, u32[]{:S(2)}, u32[]{:S(2)}) %collective-permute-start.4) | collective-permute-done | bytes 65568 | tf_op jit(solution)/shard_map/ppermute | solution.py:158
  58.7 1.3 %collective-permute-done.5.d_ref = f32[32,512]{1,0:T(8,128)S(1)} collective-permute-done((f32[32,512]{1,0:T(8,128)}, f32[32,512]{1,0:T(8,128)S(1)}, u32[]{:S(2)}, u32[]{:S(2)}) %collective-permute-start.5) | collective-permute-done | bytes 65568 | tf_op jit(solution)/shard_map/ppermute | solution.py:158
  60.6 1.7 %residual.1 = (f32[32,512]{1,0:T(8,128)}, f32[32,128]{1,0:T(8,128)}) custom-call(bf16[32,512]{1,0:T(8,128)(2,1)} %reshape.18.residual_ref, f32[32,512]{1,0:T(8,128)} %get-tuple-element.21.a_ref, f32[32,512]{1,0:T(8,128)} %copy-done.20, f32[32,512]{1,0:T(8,128)} %copy-done.21, f32[32,512]{1,0:T(8,128)} %copy-done.22), custom_call_target="tpu_custom_call" | custom-call | tf_op jit(solution)/shard_map/residual/pallas_call | solution.py:236
  62.3 2.2 %collective-permute-start.8 = (f32[32,128]{1,0:T(8,128)}, f32[32,128]{1,0:T(8,128)S(1)}, u32[]{:S(2)}, u32[]{:S(2)}) collective-permute-start(f32[32,128]{1,0:T(8,128)} %get-tuple-element.26), channel_id=1, source_target_pairs={{0,12},{1,13},{2,14},{3,15},{4,0},{5,1},{6,2},{7,3},{8,4},{9,5},{1... | collective-permute-start | bytes 49160 | tf_op jit(solution)/shard_map/ppermute | solution.py:152
  64.4 1.1 %collective-permute-start.7 = (f32[32,128]{1,0:T(8,128)}, f32[32,128]{1,0:T(8,128)S(1)}, u32[]{:S(2)}, u32[]{:S(2)}) collective-permute-start(f32[32,128]{1,0:T(8,128)} %get-tuple-element.26), channel_id=1, source_target_pairs={{0,8},{1,9},{2,10},{3,11},{4,12},{5,13},{6,14},{7,15},{8,0},{9,1},... | collective-permute-start | bytes 49160 | tf_op jit(solution)/shard_map/ppermute | solution.py:152
  66.2 3.6 %collective-permute-done.7 = f32[32,128]{1,0:T(8,128)S(1)} collective-permute-done((f32[32,128]{1,0:T(8,128)}, f32[32,128]{1,0:T(8,128)S(1)}, u32[]{:S(2)}, u32[]{:S(2)}) %collective-permute-start.7) | collective-permute-done | bytes 16416 | tf_op jit(solution)/shard_map/ppermute | solution.py:152
  71.4 2.6 %collective-permute-start.11 = (f32[32,128]{1,0:T(8,128)S(1)}, f32[32,128]{1,0:T(8,128)S(1)}, u32[]{:S(2)}, u32[]{:S(2)}) collective-permute-start(f32[32,128]{1,0:T(8,128)S(1)} %add_add_fusion), channel_id=1, source_target_pairs={{0,3},{1,0},{2,1},{3,2},{4,7},{5,4},{6,5},{7,6},{8,11},{9,8},{10,9... | collective-permute-start | bytes 49160 | tf_op jit(solution)/shard_map/ppermute | solution.py:158
  75.4 3.8 %collective-permute-done.10 = f32[32,128]{1,0:T(8,128)S(1)} collective-permute-done((f32[32,128]{1,0:T(8,128)S(1)}, f32[32,128]{1,0:T(8,128)S(1)}, u32[]{:S(2)}, u32[]{:S(2)}) %collective-permute-start.10) | collective-permute-done | bytes 16416 | tf_op jit(solution)/shard_map/ppermute | solution.py:158
  81.6 4.1 %convert_element_type.15 = f32[32,2,128,128]{3,2,1,0:T(8,128)} convert(bf16[32,2,128,128]{3,2,1,0:T(8,128)(2,1)} %all-to-all-done) | non-fusion elementwise | flops 1048576 | bytes 6291456 | tf_op jit(solution)/shard_map/convert_element_type | solution.py:250
  (65 shorter events, 13.9 us)
Async XLA Ops:
  10.9 8.9 %copy-start.1 = (f32[16,2,128,128]{3,2,1,0:T(8,128)S(1)}, f32[16,2,128,128]{3,2,1,0:T(8,128)}, u32[]{:S(2)}) copy-start(f32[16,2,128,128]{3,2,1,0:T(8,128)} %state_ref.3) | copy-start | bytes 6291460
  10.9 8.9 %copy-start.6 = (bf16[16,2,3,256]{3,1,2,0:T(2,128)(2,1)S(1)}, bf16[16,2,3,256]{3,1,2,0:T(2,128)(2,1)}, u32[]{:S(2)}) copy-start(bf16[16,2,3,256]{3,1,2,0:T(2,128)(2,1)} %param.10) | copy-start | bytes 147460
  10.9 8.9 %copy-start.8 = (f32[16]{0:T(128)S(1)}, f32[16]{0:T(128)}, u32[]{:S(2)}) copy-start(f32[16]{0:T(128)} %table_ref.3) | copy-start | bytes 196
  10.9 8.9 %copy-start.10 = (s32[2]{0:T(128)S(1)}, s32[2]{0:T(128)}, u32[]{:S(2)}) copy-start(s32[2]{0:T(128)} %index_ref.3) | copy-start | bytes 28
  10.9 8.9 %copy-start.12 = (s32[16]{0:T(128)S(1)}, s32[16]{0:T(128)}, u32[]{:S(2)}) copy-start(s32[16]{0:T(128)} %active_ref.3) | copy-start | bytes 196
  10.9 8.9 %copy-start.14 = (s32[1,16]{1,0:T(1,128)S(1)}, s32[1,16]{1,0:T(1,128)}, u32[]{:S(2)}) copy-start(s32[1,16]{1,0:T(1,128)} %slot_ref.3) | copy-start | bytes 196
  11.0 8.9 %copy-start.16 = (s32[1,16]{1,0:T(1,128)S(1)}, s32[1,16]{1,0:T(1,128)}, u32[]{:S(2)}) copy-start(s32[1,16]{1,0:T(1,128)} %dest_ref.3) | copy-start | bytes 196
  11.0 70.7 %all-to-all-start = ((bf16[32,2,128,128]{3,2,1,0:T(8,128)(2,1)}), bf16[32,2,128,128]{3,2,1,0:T(8,128)(2,1)}, u32[]{:S(2)}, u32[]{:S(2)}) async-start(bf16[32,2,128,128]{3,2,1,0:T(8,128)(2,1)} %copy-done.2), calls=%async_computation | async-start | bytes 4194304 | tf_op jit(solution)/shard_map/all_to_all | solution.py:193
  30.5 26.3 %copy-start.23 = (bf16[16,2,512]{2,1,0:T(2,128)(2,1)S(1)}, bf16[16,2,512]{2,1,0:T(2,128)(2,1)}, u32[]{:S(2)}) copy-start(bf16[16,2,512]{2,1,0:T(2,128)(2,1)} %param.11) | copy-start | bytes 98308
  30.5 44.4 %copy-start.24 = (bf16[512]{0:T(512)(128)(2,1)S(1)}, bf16[512]{0:T(512)(128)(2,1)}, u32[]{:S(2)}) copy-start(bf16[512]{0:T(512)(128)(2,1)} %param.18) | copy-start | bytes 3076
  32.2 9.6 %collective-permute-start = (f32[4,32,512]{2,1,0:T(8,128)S(1)}, f32[4,32,512]{2,1,0:T(8,128)S(1)}, u32[]{:S(2)}, u32[]{:S(2)}) collective-permute-start(f32[4,32,512]{2,1,0:T(8,128)S(1)} %get-tuple-element.18), channel_id=1, source_target_pairs={{0,4},{1,5},{2,6},{3,7},{4,8},{5,9},{6,10},{7,11},{8,12},{9,13},{1... | collective-permute-start | bytes 786440 | tf_op jit(solution)/shard_map/ppermute | solution.py:152
  33.7 14.7 %collective-permute-start.1 = (f32[4,32,512]{2,1,0:T(8,128)S(1)}, f32[4,32,512]{2,1,0:T(8,128)S(1)}, u32[]{:S(2)}, u32[]{:S(2)}) collective-permute-start(f32[4,32,512]{2,1,0:T(8,128)S(1)} %get-tuple-element.19), channel_id=1, source_target_pairs={{0,8},{1,9},{2,10},{3,11},{4,12},{5,13},{6,14},{7,15},{8,0},{9,1},... | collective-permute-start | bytes 786440 | tf_op jit(solution)/shard_map/ppermute | solution.py:152
  36.4 12.0 %collective-permute-start.2 = (f32[4,32,512]{2,1,0:T(8,128)S(1)}, f32[4,32,512]{2,1,0:T(8,128)S(1)}, u32[]{:S(2)}, u32[]{:S(2)}) collective-permute-start(f32[4,32,512]{2,1,0:T(8,128)S(1)} %get-tuple-element.20), channel_id=1, source_target_pairs={{0,12},{1,13},{2,14},{3,15},{4,0},{5,1},{6,2},{7,3},{8,4},{9,5},{1... | collective-permute-start | bytes 786440 | tf_op jit(solution)/shard_map/ppermute | solution.py:152
  41.7 6.6 %copy-start.17 = (f32[4,32,512]{2,1,0:T(8,128)}, f32[4,32,512]{2,1,0:T(8,128)S(1)}, u32[]{:S(2)}) copy-start(f32[4,32,512]{2,1,0:T(8,128)S(1)} %collective-permute-done.b_ref) | copy-start | bytes 786436
  51.0 6.5 %collective-permute-start.3 = (f32[32,512]{1,0:T(8,128)}, f32[32,512]{1,0:T(8,128)S(1)}, u32[]{:S(2)}, u32[]{:S(2)}) collective-permute-start(f32[32,512]{1,0:T(8,128)} %get-tuple-element.22), channel_id=1, source_target_pairs={{0,1},{1,2},{2,3},{3,0},{4,5},{5,6},{6,7},{7,4},{8,9},{9,10},{10,1... | collective-permute-start | bytes 196616 | tf_op jit(solution)/shard_map/ppermute | solution.py:158
  52.6 6.1 %collective-permute-start.4 = (f32[32,512]{1,0:T(8,128)}, f32[32,512]{1,0:T(8,128)S(1)}, u32[]{:S(2)}, u32[]{:S(2)}) collective-permute-start(f32[32,512]{1,0:T(8,128)} %get-tuple-element.23), channel_id=1, source_target_pairs={{0,2},{1,3},{2,0},{3,1},{4,6},{5,7},{6,4},{7,5},{8,10},{9,11},{10,... | collective-permute-start | bytes 196616 | tf_op jit(solution)/shard_map/ppermute | solution.py:158
  55.5 4.5 %collective-permute-start.5 = (f32[32,512]{1,0:T(8,128)}, f32[32,512]{1,0:T(8,128)S(1)}, u32[]{:S(2)}, u32[]{:S(2)}) collective-permute-start(f32[32,512]{1,0:T(8,128)} %get-tuple-element.24), channel_id=1, source_target_pairs={{0,3},{1,0},{2,1},{3,2},{4,7},{5,4},{6,5},{7,6},{8,11},{9,8},{10,9... | collective-permute-start | bytes 196616 | tf_op jit(solution)/shard_map/ppermute | solution.py:158
  57.5 2.5 %copy-start.20 = (f32[32,512]{1,0:T(8,128)}, f32[32,512]{1,0:T(8,128)S(1)}, u32[]{:S(2)}) copy-start(f32[32,512]{1,0:T(8,128)S(1)} %collective-permute-done.3.b_ref) | copy-start | bytes 196612
  62.3 4.0 %collective-permute-start.8 = (f32[32,128]{1,0:T(8,128)}, f32[32,128]{1,0:T(8,128)S(1)}, u32[]{:S(2)}, u32[]{:S(2)}) collective-permute-start(f32[32,128]{1,0:T(8,128)} %get-tuple-element.26), channel_id=1, source_target_pairs={{0,12},{1,13},{2,14},{3,15},{4,0},{5,1},{6,2},{7,3},{8,4},{9,5},{1... | collective-permute-start | bytes 49160 | tf_op jit(solution)/shard_map/ppermute | solution.py:152
  64.4 5.5 %collective-permute-start.7 = (f32[32,128]{1,0:T(8,128)}, f32[32,128]{1,0:T(8,128)S(1)}, u32[]{:S(2)}, u32[]{:S(2)}) collective-permute-start(f32[32,128]{1,0:T(8,128)} %get-tuple-element.26), channel_id=1, source_target_pairs={{0,8},{1,9},{2,10},{3,11},{4,12},{5,13},{6,14},{7,15},{8,0},{9,1},... | collective-permute-start | bytes 49160 | tf_op jit(solution)/shard_map/ppermute | solution.py:152
  65.6 5.2 %collective-permute-start.6 = (f32[32,128]{1,0:T(8,128)}, f32[32,128]{1,0:T(8,128)S(1)}, u32[]{:S(2)}, u32[]{:S(2)}) collective-permute-start(f32[32,128]{1,0:T(8,128)} %get-tuple-element.26), channel_id=1, source_target_pairs={{0,4},{1,5},{2,6},{3,7},{4,8},{5,9},{6,10},{7,11},{8,12},{9,13},{1... | collective-permute-start | bytes 49160 | tf_op jit(solution)/shard_map/ppermute | solution.py:152
  71.4 4.0 %collective-permute-start.11 = (f32[32,128]{1,0:T(8,128)S(1)}, f32[32,128]{1,0:T(8,128)S(1)}, u32[]{:S(2)}, u32[]{:S(2)}) collective-permute-start(f32[32,128]{1,0:T(8,128)S(1)} %add_add_fusion), channel_id=1, source_target_pairs={{0,3},{1,0},{2,1},{3,2},{4,7},{5,4},{6,5},{7,6},{8,11},{9,8},{10,9... | collective-permute-start | bytes 49160 | tf_op jit(solution)/shard_map/ppermute | solution.py:158
  74.0 5.2 %collective-permute-start.10 = (f32[32,128]{1,0:T(8,128)S(1)}, f32[32,128]{1,0:T(8,128)S(1)}, u32[]{:S(2)}, u32[]{:S(2)}) collective-permute-start(f32[32,128]{1,0:T(8,128)S(1)} %add_add_fusion), channel_id=1, source_target_pairs={{0,2},{1,3},{2,0},{3,1},{4,6},{5,7},{6,4},{7,5},{8,10},{9,11},{10,... | collective-permute-start | bytes 49160 | tf_op jit(solution)/shard_map/ppermute | solution.py:158
  74.0 5.2 %collective-permute-start.9 = (f32[32,128]{1,0:T(8,128)S(1)}, f32[32,128]{1,0:T(8,128)S(1)}, u32[]{:S(2)}, u32[]{:S(2)}) collective-permute-start(f32[32,128]{1,0:T(8,128)S(1)} %add_add_fusion), channel_id=1, source_target_pairs={{0,1},{1,2},{2,3},{3,0},{4,5},{5,6},{6,7},{7,4},{8,9},{9,10},{10,1... | collective-permute-start | bytes 49160 | tf_op jit(solution)/shard_map/ppermute | solution.py:158
  (14 other events, 13.3 us)

commit v2 on v1

v2 whole, which is shorter than its diff:
```python
import jax
import jax.numpy as jnp
from jax import lax
from jax.experimental import pallas as pl
from jax.experimental.pallas import tpu as pltpu
from jax.sharding import PartitionSpec as P

D = 8192
STEPS = 2
CAP = 2
SIDE = 4
W = 128

SMEM = pl.BlockSpec(memory_space=pltpu.SMEM)
VMEM = pl.BlockSpec(memory_space=pltpu.VMEM)
HBM = pl.BlockSpec(memory_space=pltpu.HBM)


def decay(table_ref, index_ref, h):
    return table_ref[index_ref[h]]


def rows_of(k, v, gamma, h):
    kh = k[:, h * W : (h + 1) * W]
    vh = v[:, h * W : (h + 1) * W]
    row = lax.broadcasted_iota(jnp.int32, (8, W), 0)
    first = gamma * kh[0:1]
    hi = first.astype(jnp.bfloat16).astype(jnp.float32)
    mid = (first - hi).astype(jnp.bfloat16).astype(jnp.float32)
    low = first - hi - mid
    left = jnp.where(row == 0, hi, jnp.where(row == 1, mid, jnp.where(row == 2, low, jnp.where(row == 3, kh[1:2], 0.0))))
    right = jnp.where(row < 3, vh[0:1], jnp.where(row == 3, vh[1:2], 0.0))
    return left, right


def outer(left, right):
    return lax.dot_general(
        left.astype(jnp.bfloat16),
        right.astype(jnp.bfloat16),
        (((0,), (0,)), ((), ())),
        preferred_element_type=jnp.float32,
    )


def leave_kernel(
    table_any,
    index_any,
    active_any,
    slot_any,
    dest_any,
    tok_any,
    state_any,
    out_any,
    table_ref,
    index_ref,
    active_ref,
    slot_ref,
    dest_ref,
    tok_ref,
    state_ref,
    buf_ref,
    map_ref,
    in_sem,
    out_sem,
):
    me = lax.axis_index("batch")
    entries = slot_ref.shape[1]
    heads = state_ref.shape[1]
    groups = map_ref.shape[0] // CAP
    pairs = (
        (state_any, state_ref),
        (tok_any, tok_ref),
        (slot_any, slot_ref),
        (dest_any, dest_ref),
        (active_any, active_ref),
        (table_any, table_ref),
        (index_any, index_ref),
    )
    loads = [pltpu.make_async_copy(a, b, in_sem.at[n]) for n, (a, b) in enumerate(pairs)]
    for load in loads:
        load.start()
    for n in range(map_ref.shape[0]):
        map_ref[n] = -1
    for load in loads[2:]:
        load.wait()

    def entry(j, carry):
        dest = dest_ref[0, j]
        base = dest * CAP
        taken = jnp.where(map_ref[base] >= 0, 1, 0)

        @pl.when(dest != me)
        def _():
            map_ref[base + taken] = slot_ref[0, j]

        return carry

    lax.fori_loop(0, entries, entry, 0)
    loads[1].wait()
    loads[0].wait()
    def store_of(n):
        part = pl.ds(n * CAP, CAP)
        return pltpu.make_async_copy(buf_ref.at[part], out_any.at[part], out_sem.at[n])

    def fill(n, carry):
        for position in range(CAP):
            found = map_ref[n * CAP + position]
            slot = jnp.maximum(found, 0)
            on = jnp.where(active_ref[slot] > 0, 1.0, 0.0)
            tokens = tok_ref[slot].astype(jnp.float32)
            for h in range(heads):
                gamma = decay(table_ref, index_ref, h)
                left, right = rows_of(tokens[1], tokens[2], gamma, h)
                keep = jnp.where(on > 0.0, gamma * gamma, 1.0)
                final = keep * state_ref[slot, h] + outer(left * on, right)
                final = jnp.where(found >= 0, final, 0.0)
                buf_ref[n * CAP + position, h] = final.astype(jnp.bfloat16)
        store_of(n).start()
        return carry

    lax.fori_loop(0, groups, fill, 0, unroll=2)
    for n in range(groups):
        store_of(n).wait()


def decode_kernel(
    table_any,
    index_any,
    active_any,
    slot_any,
    dest_any,
    tok_ref,
    state_ref,
    weight_any,
    after_any,
    new_ref,
    part0_any,
    part1_any,
    part2_any,
    part3_any,
    table_ref,
    index_ref,
    active_ref,
    slot_ref,
    dest_ref,
    gone_ref,
    heads_ref,
    weight_ref,
    parts_ref,
    scalar_sem,
    weight_sem,
    parts_sem,
):
    parts_any = (part0_any, part1_any, part2_any, part3_any)
    me = lax.axis_index("batch")
    entries = slot_ref.shape[1]
    heads = state_ref.shape[1]
    batch = state_ref.shape[0]
    i = pl.program_id(0)
    load = pltpu.make_async_copy(weight_any, weight_ref, weight_sem)

    @pl.when(i == 0)
    def _():
        pairs = (
            (table_any, table_ref),
            (index_any, index_ref),
            (active_any, active_ref),
            (slot_any, slot_ref),
            (dest_any, dest_ref),
        )
        copies = [pltpu.make_async_copy(a, b, scalar_sem.at[n]) for n, (a, b) in enumerate(pairs)]
        for copy in copies:
            copy.start()
        load.start()
        for copy in copies:
            copy.wait()
        for s in range(gone_ref.shape[0]):
            gone_ref[s] = 0
        for j in range(entries):
            slot = slot_ref[0, j]
            moves = jnp.where(dest_ref[0, j] != me, 1, 0)
            gone_ref[slot] = gone_ref[slot] + moves

    row = lax.broadcasted_iota(jnp.int32, (8, W), 0)
    wide = lax.broadcasted_iota(jnp.int32, (8, 2 * W), 0)
    lane = lax.broadcasted_iota(jnp.int32, (8, 2 * W), 1)
    ones = jnp.where((wide == 4) & (lane < W), 1.0, jnp.where((wide == 5) & (lane >= W), 1.0, 0.0))
    for b in range(batch):
        r = i * batch + b
        on = active_ref[r] > 0
        gone = gone_ref[r] > 0
        tokens = tok_ref[b].astype(jnp.float32)
        query, key, value = tokens[0], tokens[1], tokens[2]
        for h in range(heads):
            part = slice(h * W, (h + 1) * W)
            q, k, v = query[:, part], key[:, part], value[:, part]
            gamma = decay(table_ref, index_ref, h)
            left, right = rows_of(key, value, gamma, h)
            left = jnp.where(row == 4, q[0:1], jnp.where(row == 5, q[1:2], left))
            mixed = outer(left, jnp.concatenate([right, ones], axis=1))
            before = state_ref[b, h]
            raw1 = gamma * jnp.sum(mixed[:, W : 2 * W] * before, axis=0, keepdims=True)
            raw1 = raw1 + jnp.sum(q[0:1] * k[0:1], axis=1, keepdims=True) * v[0:1]
            final = (gamma * gamma) * before + mixed[:, :W]
            raw2 = jnp.sum(mixed[:, 2 * W :] * final, axis=0, keepdims=True)
            raw = jnp.where(row == 0, raw1, jnp.where(row == 1, raw2, 0.0))
            scaled = raw * lax.rsqrt(jnp.mean(raw * raw, axis=1, keepdims=True) + 1e-06)
            heads_ref[r, :, part] = jnp.where(on, scaled, 0.0)
            final = jnp.where(on, final, before)
            new_ref[b, h] = jnp.where(gone, 0.0, final)

    @pl.when(i == pl.num_programs(0) - 1)
    def _():
        count, padded, depth = heads_ref.shape
        rows = count * STEPS
        line = lax.broadcasted_iota(jnp.int32, (rows, count * padded), 0)
        source = lax.broadcasted_iota(jnp.int32, (rows, count * padded), 1)
        pick = jnp.where(source == (line // STEPS) * padded + line % STEPS, 1.0, 0.0).astype(jnp.bfloat16)
        out = heads_ref[...].reshape(count * padded, depth).astype(jnp.bfloat16)
        out = jnp.dot(pick, out, preferred_element_type=jnp.float32).astype(jnp.bfloat16)
        load.wait()
        share = parts_ref.shape[3]
        column = lax.axis_index("tensor")
        stores = []
        for dx in (1, 2, 3, 0):
            for dy in range(SIDE):
                block = lax.rem(column // SIDE + dx, SIDE) * SIDE + lax.rem(column + dy, SIDE)
                weight = weight_ref[:, pl.ds(pl.multiple_of(block * share, share), share)]
                parts_ref[dx, dy] = jnp.dot(out, weight, preferred_element_type=jnp.float32)
            stores.append(pltpu.make_async_copy(parts_ref.at[dx], parts_any[dx], parts_sem.at[dx]))
            stores[-1].start()
        for store in stores:
            store.wait()


def add_kernel(a_ref, b_ref, c_ref, d_ref, *out_refs):
    for dy in range(SIDE):
        out_refs[dy][...] = (a_ref[dy] + b_ref[dy]) + (c_ref[dy] + d_ref[dy])


def residual_kernel(a_ref, b_ref, c_ref, d_ref, residual_ref, hsum_ref, square_ref):
    total = (a_ref[...] + b_ref[...]) + (c_ref[...] + d_ref[...])
    residual = residual_ref[...].astype(jnp.float32)
    hsum = jnp.concatenate([residual[r] for r in range(residual.shape[0])], axis=0) + total
    hsum_ref[...] = hsum
    square_ref[...] = jnp.broadcast_to(jnp.sum(hsum * hsum, axis=1, keepdims=True), square_ref.shape)


def norm_kernel(hsum_ref, a_ref, b_ref, c_ref, d_ref, gain_ref, normed_ref, residual_ref):
    total = (a_ref[...] + b_ref[...]) + (c_ref[...] + d_ref[...])
    hsum = hsum_ref[...]
    normed = hsum * lax.rsqrt(total[:, :1] / D + 1e-05) * gain_ref[...].astype(jnp.float32)
    for r in range(normed_ref.shape[0]):
        part = slice(r * STEPS, (r + 1) * STEPS)
        normed_ref[r] = normed[part].astype(jnp.bfloat16)
        residual_ref[r] = hsum[part].astype(jnp.bfloat16)


def widen_kernel(landed_any, arrived_any, in_ref, wide_ref, in_sem, out_sem):
    chunks, size = in_ref.shape[:2]
    loads, stores = [], []
    for n in range(chunks):
        part = pl.ds(n * size, size)
        loads.append(pltpu.make_async_copy(landed_any.at[part], in_ref.at[n], in_sem.at[n]))
        loads[n].start()
        stores.append(pltpu.make_async_copy(wide_ref.at[n], arrived_any.at[part], out_sem.at[n]))
    for n in range(chunks):
        loads[n].wait()
        wide_ref[n] = in_ref[n].astype(jnp.float32)
        stores[n].start()
    for store in stores:
        store.wait()


def shift_x(value, d):
    return lax.ppermute(
        value, "tensor", [(x * SIDE + y, ((x + d) % SIDE) * SIDE + y) for x in range(SIDE) for y in range(SIDE)]
    )


def shift_y(value, d):
    return lax.ppermute(
        value, "tensor", [(x * SIDE + y, x * SIDE + (y + d) % SIDE) for x in range(SIDE) for y in range(SIDE)]
    )


def here(value):
    return pltpu.with_memory_space_constraint(value, pltpu.HBM)


def params(mib=24):
    return pltpu.CompilerParams(vmem_limit_bytes=mib << 20)


def body(
    tokens_qkv,
    residual_in,
    state,
    decay_table,
    decay_index,
    active,
    move_slot,
    move_dest,
    norm_gain,
    out_weight,
):
    count, heads, width, _ = state.shape
    groups = lax.axis_size("batch")
    rows = count * STEPS
    share = residual_in.shape[2]
    f32, bf16 = jnp.float32, jnp.bfloat16
    pair = (CAP, heads, width, width)
    tokens = jnp.transpose(tokens_qkv, (0, 2, 1, 3))
    scalar_scratch = [
        pltpu.SMEM(decay_table.shape, f32),
        pltpu.SMEM(decay_index.shape, jnp.int32),
        pltpu.SMEM(active.shape, jnp.int32),
        pltpu.SMEM(move_slot.shape, jnp.int32),
        pltpu.SMEM(move_dest.shape, jnp.int32),
    ]
    scalars = (decay_table, decay_index, active, move_slot, move_dest)
    dma = pltpu.SemaphoreType.DMA

    moved = (groups * CAP,) + pair[1:]
    leaving = pl.pallas_call(
        leave_kernel,
        out_shape=pltpu.HBM(moved, bf16),
        in_specs=[HBM] * 7,
        out_specs=HBM,
        scratch_shapes=[
            *scalar_scratch,
            pltpu.VMEM(tokens.shape, bf16),
            pltpu.VMEM(state.shape, f32),
            pltpu.VMEM(moved, bf16),
            pltpu.SMEM((groups * CAP,), jnp.int32),
            dma((7,)),
            dma((groups,)),
        ],
        compiler_params=params(),
        cost_estimate=pl.CostEstimate(flops=32 * 20 * width * width, bytes_accessed=8 << 20, transcendentals=0),
        name="leave",
    )(*(here(value) for value in (*scalars, tokens, state)))
    landed = lax.all_to_all(leaving, "batch", split_axis=0, concat_axis=0, tiled=True)

    grid = 4
    new_state, *parts = pl.pallas_call(
        decode_kernel,
        grid=(grid,),
        out_shape=(
            pltpu.HBM(state.shape, f32),
            *[pltpu.HBM((SIDE, rows, share), f32)] * SIDE,
        ),
        in_specs=[HBM] * 5
        + [
            pl.BlockSpec((count // grid, 3, STEPS, heads * width), lambda i: (i, 0, 0, 0)),
            pl.BlockSpec((count // grid, heads, width, width), lambda i: (i, 0, 0, 0)),
            HBM,
            HBM,
        ],
        out_specs=(pl.BlockSpec((count // grid, heads, width, width), lambda i: (i, 0, 0, 0)), *[HBM] * SIDE),
        scratch_shapes=[
            *scalar_scratch,
            pltpu.SMEM((count,), jnp.int32),
            pltpu.VMEM((count, 8, heads * width), f32),
            pltpu.VMEM(out_weight.shape, bf16),
            pltpu.VMEM((SIDE, SIDE, rows, share), f32),
            dma((5,)),
            dma,
            dma((SIDE,)),
        ],
        compiler_params=params(),
        cost_estimate=pl.CostEstimate(flops=32 * 20 * width * width, bytes_accessed=8 << 20, transcendentals=0),
        name="decode",
    )(*(here(value) for value in (*scalars, tokens, state, out_weight, leaving)))

    lines = [parts[0]] + [shift_x(parts[d], d) for d in range(1, SIDE)]
    sums = pl.pallas_call(
        add_kernel,
        out_shape=[jax.ShapeDtypeStruct((rows, share), f32)] * SIDE,
        in_specs=[VMEM] * SIDE,
        out_specs=[VMEM] * SIDE,
        compiler_params=params(),
        name="add",
    )(*lines)
    terms = [sums[0]] + [shift_y(sums[d], d) for d in range(1, SIDE)]
    hsum, square = pl.pallas_call(
        residual_kernel,
        out_shape=(jax.ShapeDtypeStruct((rows, share), f32), jax.ShapeDtypeStruct((rows, W), f32)),
        in_specs=[VMEM] * (SIDE + 1),
        out_specs=(VMEM, VMEM),
        compiler_params=params(),
        name="residual",
    )(*terms, residual_in)
    square = square + (shift_x(square, 1) + shift_x(square, 2) + shift_x(square, 3))
    squares = [square] + [shift_y(square, d) for d in range(1, SIDE)]
    normed, residual_out = pl.pallas_call(
        norm_kernel,
        out_shape=[jax.ShapeDtypeStruct(residual_in.shape, bf16)] * 2,
        in_specs=[VMEM] * (SIDE + 2),
        out_specs=[VMEM] * 2,
        compiler_params=params(),
        name="norm",
    )(hsum, *squares, norm_gain.reshape(1, share))
    chunks = groups // 2
    arrived = pl.pallas_call(
        widen_kernel,
        out_shape=pltpu.HBM(moved, f32),
        in_specs=[pl.BlockSpec(memory_space=pl.ANY)],
        out_specs=HBM,
        scratch_shapes=[
            pltpu.VMEM((chunks, moved[0] // chunks) + pair[1:], bf16),
            pltpu.VMEM((chunks, moved[0] // chunks) + pair[1:], f32),
            dma((chunks,)),
            dma((chunks,)),
        ],
        compiler_params=params(),
        name="widen",
    )(landed)
    return (normed, residual_out, new_state, arrived)


def solution(mesh):
    return jax.shard_map(
        body,
        mesh=mesh,
        in_specs=(
            P("batch", None, None, "tensor"),
            P("batch", None, "tensor"),
            P("batch", "tensor", None, None),
            P(),
            P("tensor"),
            P("batch"),
            P("batch", None),
            P("batch", None),
            P("tensor"),
            P("tensor", None),
        ),
        out_specs=(
            P("batch", None, "tensor"),
            P("batch", None, "tensor"),
            P("batch", "tensor", None, None),
            P("batch", "tensor", None, None),
        ),
        check_vma=False,
    )
```

time: 86.5 us -> 66.9 us (0.77)
  the two profiles are of different devices: /device:TPU:32 before, /device:TPU:1 now
where the time goes in v2:
time: 66.9 us; the launch traced here: 66.7 us
  starting transfers between devices  27.5 us (41%)
  waiting for transfers between devices  22.1 us (33%)
  Pallas kernels  15.4 us (23%)
  local copies, waits for them, and re-layouts  0.97 us (1%)
  between operations  0.68 us (1%)
    ppermute x6, waiting for transfers between devices, shift_x(): lax.ppermute(value, 'tensor', [(x * SIDE + y, (x + d) % SIDE * SIDE + y)...  12.8 us
    all_to_all x1, starting transfers between devices, body(): lax.all_to_all(leaving, 'batch', split_axis=0, concat_axis=0, tiled=True)  10 us
    ppermute x6, starting transfers between devices, shift_x(): lax.ppermute(value, 'tensor', [(x * SIDE + y, (x + d) % SIDE * SIDE + y)...  9.38 us
    ppermute x6, starting transfers between devices, shift_y(): lax.ppermute(value, 'tensor', [(x * SIDE + y, x * SIDE + (y + d) % SIDE)...  8.15 us
    pallas_call x1, Pallas kernels, body(): pl.pallas_call(decode_kernel, grid=(grid,), out_shape=(pltpu.HBM(state.sh...  7.43 us
    ppermute x6, waiting for transfers between devices, shift_y(): lax.ppermute(value, 'tensor', [(x * SIDE + y, x * SIDE + (y + d) % SIDE)...  6.1 us
    pallas_call x1, Pallas kernels, body(): pl.pallas_call(leave_kernel, out_shape=pltpu.HBM(moved, bf16), in_specs=[...  4.76 us
    all_to_all x1, waiting for transfers between devices, body(): lax.all_to_all(leaving, 'batch', split_axis=0, concat_axis=0, tiled=True)  3.15 us
  transfers between devices with their start and end apart: 13, of which 10 were waited for; matrix products, arithmetic and copies ran while one was open for 0% of the time, Pallas kernels for 12%

profile of v2, /device:TPU:1, one launch (start us, length us, event | category | flops | bytes accessed | tf_op | source)
XLA Modules:
  0.0 66.7 jit_solution(5094329067277318137)
XLA Ops:
  0.6 4.8 %leave.1.after_any = bf16[32,2,128,128]{3,2,1,0:T(8,128)(2,1)} custom-call(f32[16]{0:T(128)} %table_any.3, s32[2]{0:T(128)} %index_any.3, s32[16]{0:T(128)} %active_any.3, s32[1,16]{1,0:T(1,128)} %slot_any.3, s32[1,16]{1,0:T(1,128)} %dest_any.3, bf16[16,3,2,256]{3,2,1,0:T(2,128)(2,1)} %bitcast.1, f32[16,2,128,128]{3,2,1,0:T(8,128)} %state_ref.1), custom_call_target="tpu_custom_call" | custom-call | flops 10485760 | bytes 8388608 | tf_op jit(solution)/shard_map/leave/pallas_call | solution.py:325
  5.4 10.0 %all-to-all-start = ((bf16[32,2,128,128]{3,2,1,0:T(8,128)(2,1)}), bf16[32,2,128,128]{3,2,1,0:T(8,128)(2,1)S(1)}, u32[]{:S(2)}, u32[]{:S(2)}) async-start(bf16[32,2,128,128]{3,2,1,0:T(8,128)(2,1)} %leave.1.after_any), calls=%async_computation | async-start | bytes 4194304 | tf_op jit(solution)/shard_map/all_to_all | solution.py:343
  15.4 7.4 %decode.1 = (f32[16,2,128,128]{3,2,1,0:T(8,128)}, f32[4,32,512]{2,1,0:T(8,128)}, f32[4,32,512]{2,1,0:T(8,128)}, f32[4,32,512]{2,1,0:T(8,128)}, f32[4,32,512]{2,1,0:T(8,128)}) custom-call(f32[16]{0:T(128)} %table_any.3, s32[2]{0:T(128)} %index_any.3, s32[16]{0:T(128)} %active_any.3, s32[1,16]{1,0:T(1,128)} %slot_any.3, s32[1,16]{1,0:T(1,128)} %dest_any.3, ...), custom_call_target="tpu_custom_call" | custom-call | flops 10485760 | bytes 8388608 | tf_op jit(solution)/shard_map/decode/pallas_call | solution.py:346
  22.9 1.3 %collective-permute-start = (f32[4,32,512]{2,1,0:T(8,128)}, f32[4,32,512]{2,1,0:T(8,128)S(1)}, u32[]{:S(2)}, u32[]{:S(2)}) collective-permute-start(f32[4,32,512]{2,1,0:T(8,128)} %get-tuple-element.18), channel_id=1, source_target_pairs={{0,4},{1,5},{2,6},{3,7},{4,8},{5,9},{6,10},{7,11},{8,12},{9,13},{1... | collective-permute-start | bytes 786440 | tf_op jit(solution)/shard_map/ppermute | solution.py:276
  24.2 2.5 %collective-permute-start.1 = (f32[4,32,512]{2,1,0:T(8,128)}, f32[4,32,512]{2,1,0:T(8,128)S(1)}, u32[]{:S(2)}, u32[]{:S(2)}) collective-permute-start(f32[4,32,512]{2,1,0:T(8,128)} %get-tuple-element.19), channel_id=1, source_target_pairs={{0,8},{1,9},{2,10},{3,11},{4,12},{5,13},{6,14},{7,15},{8,0},{9,1},... | collective-permute-start | bytes 786440 | tf_op jit(solution)/shard_map/ppermute | solution.py:276
  26.6 1.2 %collective-permute-start.2 = (f32[4,32,512]{2,1,0:T(8,128)}, f32[4,32,512]{2,1,0:T(8,128)S(1)}, u32[]{:S(2)}, u32[]{:S(2)}) collective-permute-start(f32[4,32,512]{2,1,0:T(8,128)} %get-tuple-element.20), channel_id=1, source_target_pairs={{0,12},{1,13},{2,14},{3,15},{4,0},{5,1},{6,2},{7,3},{8,4},{9,5},{1... | collective-permute-start | bytes 786440 | tf_op jit(solution)/shard_map/ppermute | solution.py:276
  27.8 4.4 %collective-permute-done.b_ref = f32[4,32,512]{2,1,0:T(8,128)S(1)} collective-permute-done((f32[4,32,512]{2,1,0:T(8,128)}, f32[4,32,512]{2,1,0:T(8,128)S(1)}, u32[]{:S(2)}, u32[]{:S(2)}) %collective-permute-start) | collective-permute-done | bytes 262176 | tf_op jit(solution)/shard_map/ppermute | solution.py:276
  32.2 6.6 %collective-permute-done.1.c_ref = f32[4,32,512]{2,1,0:T(8,128)S(1)} collective-permute-done((f32[4,32,512]{2,1,0:T(8,128)}, f32[4,32,512]{2,1,0:T(8,128)S(1)}, u32[]{:S(2)}, u32[]{:S(2)}) %collective-permute-start.1) | collective-permute-done | bytes 262176 | tf_op jit(solution)/shard_map/ppermute | solution.py:276
  38.8 0.9 %copy-done = f32[4,32,512]{2,1,0:T(8,128)S(1)} copy-done((f32[4,32,512]{2,1,0:T(8,128)S(1)}, f32[4,32,512]{2,1,0:T(8,128)}, u32[]{:S(2)}) %copy-start) | copy-done | bytes 262168
  39.8 1.4 %collective-permute-start.3 = (f32[32,512]{1,0:T(8,128)S(1)}, f32[32,512]{1,0:T(8,128)S(1)}, u32[]{:S(2)}, u32[]{:S(2)}) collective-permute-start(f32[32,512]{1,0:T(8,128)S(1)} %get-tuple-element.22), channel_id=1, source_target_pairs={{0,1},{1,2},{2,3},{3,0},{4,5},{5,6},{6,7},{7,4},{8,9},{9,10},{10,1... | collective-permute-start | bytes 196616 | tf_op jit(solution)/shard_map/ppermute | solution.py:282
  41.2 2.6 %collective-permute-start.4 = (f32[32,512]{1,0:T(8,128)S(1)}, f32[32,512]{1,0:T(8,128)S(1)}, u32[]{:S(2)}, u32[]{:S(2)}) collective-permute-start(f32[32,512]{1,0:T(8,128)S(1)} %get-tuple-element.23), channel_id=1, source_target_pairs={{0,2},{1,3},{2,0},{3,1},{4,6},{5,7},{6,4},{7,5},{8,10},{9,11},{10,... | collective-permute-start | bytes 196616 | tf_op jit(solution)/shard_map/ppermute | solution.py:282
  43.8 1.1 %collective-permute-start.5 = (f32[32,512]{1,0:T(8,128)S(1)}, f32[32,512]{1,0:T(8,128)S(1)}, u32[]{:S(2)}, u32[]{:S(2)}) collective-permute-start(f32[32,512]{1,0:T(8,128)S(1)} %get-tuple-element.24), channel_id=1, source_target_pairs={{0,3},{1,0},{2,1},{3,2},{4,7},{5,4},{6,5},{7,6},{8,11},{9,8},{10,9... | collective-permute-start | bytes 196616 | tf_op jit(solution)/shard_map/ppermute | solution.py:282
  44.9 1.5 %collective-permute-done.4.c_ref = f32[32,512]{1,0:T(8,128)S(1)} collective-permute-done((f32[32,512]{1,0:T(8,128)S(1)}, f32[32,512]{1,0:T(8,128)S(1)}, u32[]{:S(2)}, u32[]{:S(2)}) %collective-permute-start.4) | collective-permute-done | bytes 65568 | tf_op jit(solution)/shard_map/ppermute | solution.py:282
  46.4 1.1 %collective-permute-done.5.d_ref = f32[32,512]{1,0:T(8,128)S(1)} collective-permute-done((f32[32,512]{1,0:T(8,128)S(1)}, f32[32,512]{1,0:T(8,128)S(1)}, u32[]{:S(2)}, u32[]{:S(2)}) %collective-permute-start.5) | collective-permute-done | bytes 65568 | tf_op jit(solution)/shard_map/ppermute | solution.py:282
  47.6 1.1 %collective-permute-start.6 = (f32[32,128]{1,0:T(8,128)S(1)}, f32[32,128]{1,0:T(8,128)S(1)}, u32[]{:S(2)}, u32[]{:S(2)}) collective-permute-start(f32[32,128]{1,0:T(8,128)S(1)} %get-tuple-element.26), channel_id=1, source_target_pairs={{0,4},{1,5},{2,6},{3,7},{4,8},{5,9},{6,10},{7,11},{8,12},{9,13},{1... | collective-permute-start | bytes 49160 | tf_op jit(solution)/shard_map/ppermute | solution.py:276
  48.6 2.3 %collective-permute-start.7 = (f32[32,128]{1,0:T(8,128)S(1)}, f32[32,128]{1,0:T(8,128)S(1)}, u32[]{:S(2)}, u32[]{:S(2)}) collective-permute-start(f32[32,128]{1,0:T(8,128)S(1)} %get-tuple-element.26), channel_id=1, source_target_pairs={{0,8},{1,9},{2,10},{3,11},{4,12},{5,13},{6,14},{7,15},{8,0},{9,1},... | collective-permute-start | bytes 49160 | tf_op jit(solution)/shard_map/ppermute | solution.py:276
  50.9 1.1 %collective-permute-start.8 = (f32[32,128]{1,0:T(8,128)S(1)}, f32[32,128]{1,0:T(8,128)S(1)}, u32[]{:S(2)}, u32[]{:S(2)}) collective-permute-start(f32[32,128]{1,0:T(8,128)S(1)} %get-tuple-element.26), channel_id=1, source_target_pairs={{0,12},{1,13},{2,14},{3,15},{4,0},{5,1},{6,2},{7,3},{8,4},{9,5},{1... | collective-permute-start | bytes 49160 | tf_op jit(solution)/shard_map/ppermute | solution.py:276
  52.0 1.0 %collective-permute-done.7 = f32[32,128]{1,0:T(8,128)S(1)} collective-permute-done((f32[32,128]{1,0:T(8,128)S(1)}, f32[32,128]{1,0:T(8,128)S(1)}, u32[]{:S(2)}, u32[]{:S(2)}) %collective-permute-start.7) | collective-permute-done | bytes 16416 | tf_op jit(solution)/shard_map/ppermute | solution.py:276
  53.8 1.6 %collective-permute-start.10 = (f32[32,128]{1,0:T(8,128)S(1)}, f32[32,128]{1,0:T(8,128)S(1)}, u32[]{:S(2)}, u32[]{:S(2)}) collective-permute-start(f32[32,128]{1,0:T(8,128)S(1)} %add_add_fusion.a_ref), channel_id=1, source_target_pairs={{0,2},{1,3},{2,0},{3,1},{4,6},{5,7},{6,4},{7,5},{8,10},{9,11},{10,... | collective-permute-start | bytes 49160 | tf_op jit(solution)/shard_map/ppermute | solution.py:282
  55.4 1.0 %collective-permute-start.11 = (f32[32,128]{1,0:T(8,128)S(1)}, f32[32,128]{1,0:T(8,128)S(1)}, u32[]{:S(2)}, u32[]{:S(2)}) collective-permute-start(f32[32,128]{1,0:T(8,128)S(1)} %add_add_fusion.a_ref), channel_id=1, source_target_pairs={{0,3},{1,0},{2,1},{3,2},{4,7},{5,4},{6,5},{7,6},{8,11},{9,8},{10,9... | collective-permute-start | bytes 49160 | tf_op jit(solution)/shard_map/ppermute | solution.py:282
  56.9 1.3 %collective-permute-done.10.c_ref = f32[32,128]{1,0:T(8,128)S(1)} collective-permute-done((f32[32,128]{1,0:T(8,128)S(1)}, f32[32,128]{1,0:T(8,128)S(1)}, u32[]{:S(2)}, u32[]{:S(2)}) %collective-permute-start.10) | collective-permute-done | bytes 16416 | tf_op jit(solution)/shard_map/ppermute | solution.py:282
  58.3 2.2 %collective-permute-done.9.b_ref = f32[32,128]{1,0:T(8,128)S(1)} collective-permute-done((f32[32,128]{1,0:T(8,128)S(1)}, f32[32,128]{1,0:T(8,128)S(1)}, u32[]{:S(2)}, u32[]{:S(2)}) %collective-permute-start.9) | collective-permute-done | bytes 16416 | tf_op jit(solution)/shard_map/ppermute | solution.py:282
  61.2 3.2 %all-to-all-done.landed_any = bf16[32,2,128,128]{3,2,1,0:T(8,128)(2,1)S(1)} async-done(((bf16[32,2,128,128]{3,2,1,0:T(8,128)(2,1)}), bf16[32,2,128,128]{3,2,1,0:T(8,128)(2,1)S(1)}, u32[]{:S(2)}, u32[]{:S(2)}) %all-to-all-start) | async-done | bytes 2097184 | tf_op jit(solution)/shard_map/all_to_all | solution.py:343
  64.3 2.3 %widen.1 = f32[32,2,128,128]{3,2,1,0:T(8,128)} custom-call(bf16[32,2,128,128]{3,2,1,0:T(8,128)(2,1)S(1)} %all-to-all-done.landed_any), custom_call_target="tpu_custom_call" | custom-call | tf_op jit(solution)/shard_map/widen/pallas_call | solution.py:405
  (16 shorter events, 2.3 us)
Async XLA Ops:
  5.4 58.9 %all-to-all-start = ((bf16[32,2,128,128]{3,2,1,0:T(8,128)(2,1)}), bf16[32,2,128,128]{3,2,1,0:T(8,128)(2,1)S(1)}, u32[]{:S(2)}, u32[]{:S(2)}) async-start(bf16[32,2,128,128]{3,2,1,0:T(8,128)(2,1)} %leave.1.after_any), calls=%async_computation | async-start | bytes 4194304 | tf_op jit(solution)/shard_map/all_to_all | solution.py:343
  15.4 32.0 %copy-start.1 = (bf16[16,2,512]{2,1,0:T(2,128)(2,1)S(1)}, bf16[16,2,512]{2,1,0:T(2,128)(2,1)}, u32[]{:S(2)}) copy-start(bf16[16,2,512]{2,1,0:T(2,128)(2,1)} %residual_ref.1) | copy-start | bytes 98308
  15.4 41.5 %copy-start.2 = (bf16[512]{0:T(512)(128)(2,1)S(1)}, bf16[512]{0:T(512)(128)(2,1)}, u32[]{:S(2)}) copy-start(bf16[512]{0:T(512)(128)(2,1)} %param.18) | copy-start | bytes 3076
  22.9 9.4 %collective-permute-start = (f32[4,32,512]{2,1,0:T(8,128)}, f32[4,32,512]{2,1,0:T(8,128)S(1)}, u32[]{:S(2)}, u32[]{:S(2)}) collective-permute-start(f32[4,32,512]{2,1,0:T(8,128)} %get-tuple-element.18), channel_id=1, source_target_pairs={{0,4},{1,5},{2,6},{3,7},{4,8},{5,9},{6,10},{7,11},{8,12},{9,13},{1... | collective-permute-start | bytes 786440 | tf_op jit(solution)/shard_map/ppermute | solution.py:276
  24.2 14.7 %collective-permute-start.1 = (f32[4,32,512]{2,1,0:T(8,128)}, f32[4,32,512]{2,1,0:T(8,128)S(1)}, u32[]{:S(2)}, u32[]{:S(2)}) collective-permute-start(f32[4,32,512]{2,1,0:T(8,128)} %get-tuple-element.19), channel_id=1, source_target_pairs={{0,8},{1,9},{2,10},{3,11},{4,12},{5,13},{6,14},{7,15},{8,0},{9,1},... | collective-permute-start | bytes 786440 | tf_op jit(solution)/shard_map/ppermute | solution.py:276
  26.6 12.2 %collective-permute-start.2 = (f32[4,32,512]{2,1,0:T(8,128)}, f32[4,32,512]{2,1,0:T(8,128)S(1)}, u32[]{:S(2)}, u32[]{:S(2)}) collective-permute-start(f32[4,32,512]{2,1,0:T(8,128)} %get-tuple-element.20), channel_id=1, source_target_pairs={{0,12},{1,13},{2,14},{3,15},{4,0},{5,1},{6,2},{7,3},{8,4},{9,5},{1... | collective-permute-start | bytes 786440 | tf_op jit(solution)/shard_map/ppermute | solution.py:276
  38.8 1.0 %copy-start = (f32[4,32,512]{2,1,0:T(8,128)S(1)}, f32[4,32,512]{2,1,0:T(8,128)}, u32[]{:S(2)}) copy-start(f32[4,32,512]{2,1,0:T(8,128)} %get-tuple-element.17.a_ref) | copy-start | bytes 786436
  39.8 5.1 %collective-permute-start.3 = (f32[32,512]{1,0:T(8,128)S(1)}, f32[32,512]{1,0:T(8,128)S(1)}, u32[]{:S(2)}, u32[]{:S(2)}) collective-permute-start(f32[32,512]{1,0:T(8,128)S(1)} %get-tuple-element.22), channel_id=1, source_target_pairs={{0,1},{1,2},{2,3},{3,0},{4,5},{5,6},{6,7},{7,4},{8,9},{9,10},{10,1... | collective-permute-start | bytes 196616 | tf_op jit(solution)/shard_map/ppermute | solution.py:282
  41.2 5.2 %collective-permute-start.4 = (f32[32,512]{1,0:T(8,128)S(1)}, f32[32,512]{1,0:T(8,128)S(1)}, u32[]{:S(2)}, u32[]{:S(2)}) collective-permute-start(f32[32,512]{1,0:T(8,128)S(1)} %get-tuple-element.23), channel_id=1, source_target_pairs={{0,2},{1,3},{2,0},{3,1},{4,6},{5,7},{6,4},{7,5},{8,10},{9,11},{10,... | collective-permute-start | bytes 196616 | tf_op jit(solution)/shard_map/ppermute | solution.py:282
  43.8 3.6 %collective-permute-start.5 = (f32[32,512]{1,0:T(8,128)S(1)}, f32[32,512]{1,0:T(8,128)S(1)}, u32[]{:S(2)}, u32[]{:S(2)}) collective-permute-start(f32[32,512]{1,0:T(8,128)S(1)} %get-tuple-element.24), channel_id=1, source_target_pairs={{0,3},{1,0},{2,1},{3,2},{4,7},{5,4},{6,5},{7,6},{8,11},{9,8},{10,9... | collective-permute-start | bytes 196616 | tf_op jit(solution)/shard_map/ppermute | solution.py:282
  47.6 4.5 %collective-permute-start.6 = (f32[32,128]{1,0:T(8,128)S(1)}, f32[32,128]{1,0:T(8,128)S(1)}, u32[]{:S(2)}, u32[]{:S(2)}) collective-permute-start(f32[32,128]{1,0:T(8,128)S(1)} %get-tuple-element.26), channel_id=1, source_target_pairs={{0,4},{1,5},{2,6},{3,7},{4,8},{5,9},{6,10},{7,11},{8,12},{9,13},{1... | collective-permute-start | bytes 49160 | tf_op jit(solution)/shard_map/ppermute | solution.py:276
  48.6 4.4 %collective-permute-start.7 = (f32[32,128]{1,0:T(8,128)S(1)}, f32[32,128]{1,0:T(8,128)S(1)}, u32[]{:S(2)}, u32[]{:S(2)}) collective-permute-start(f32[32,128]{1,0:T(8,128)S(1)} %get-tuple-element.26), channel_id=1, source_target_pairs={{0,8},{1,9},{2,10},{3,11},{4,12},{5,13},{6,14},{7,15},{8,0},{9,1},... | collective-permute-start | bytes 49160 | tf_op jit(solution)/shard_map/ppermute | solution.py:276
  50.9 2.9 %collective-permute-start.8 = (f32[32,128]{1,0:T(8,128)S(1)}, f32[32,128]{1,0:T(8,128)S(1)}, u32[]{:S(2)}, u32[]{:S(2)}) collective-permute-start(f32[32,128]{1,0:T(8,128)S(1)} %get-tuple-element.26), channel_id=1, source_target_pairs={{0,12},{1,13},{2,14},{3,15},{4,0},{5,1},{6,2},{7,3},{8,4},{9,5},{1... | collective-permute-start | bytes 49160 | tf_op jit(solution)/shard_map/ppermute | solution.py:276
  53.8 4.4 %collective-permute-start.10 = (f32[32,128]{1,0:T(8,128)S(1)}, f32[32,128]{1,0:T(8,128)S(1)}, u32[]{:S(2)}, u32[]{:S(2)}) collective-permute-start(f32[32,128]{1,0:T(8,128)S(1)} %add_add_fusion.a_ref), channel_id=1, source_target_pairs={{0,2},{1,3},{2,0},{3,1},{4,6},{5,7},{6,4},{7,5},{8,10},{9,11},{10,... | collective-permute-start | bytes 49160 | tf_op jit(solution)/shard_map/ppermute | solution.py:282
  55.4 2.9 %collective-permute-start.11 = (f32[32,128]{1,0:T(8,128)S(1)}, f32[32,128]{1,0:T(8,128)S(1)}, u32[]{:S(2)}, u32[]{:S(2)}) collective-permute-start(f32[32,128]{1,0:T(8,128)S(1)} %add_add_fusion.a_ref), channel_id=1, source_target_pairs={{0,3},{1,0},{2,1},{3,2},{4,7},{5,4},{6,5},{7,6},{8,11},{9,8},{10,9... | collective-permute-start | bytes 49160 | tf_op jit(solution)/shard_map/ppermute | solution.py:282
  56.4 4.1 %collective-permute-start.9 = (f32[32,128]{1,0:T(8,128)S(1)}, f32[32,128]{1,0:T(8,128)S(1)}, u32[]{:S(2)}, u32[]{:S(2)}) collective-permute-start(f32[32,128]{1,0:T(8,128)S(1)} %add_add_fusion.a_ref), channel_id=1, source_target_pairs={{0,1},{1,2},{2,3},{3,0},{4,5},{5,6},{6,7},{7,4},{8,9},{9,10},{10,1... | collective-permute-start | bytes 49160 | tf_op jit(solution)/shard_map/ppermute | solution.py:282

commit v3 on v2

--- a/solution.py
+++ b/solution.py
@@ -7,6 +7,7 @@
 
 D = 8192
 STEPS = 2
+PAIR = 2
 CAP = 2
 SIDE = 4
 W = 128
@@ -20,17 +21,47 @@
     return table_ref[index_ref[h]]
 
 
-def rows_of(k, v, gamma, h):
-    kh = k[:, h * W : (h + 1) * W]
-    vh = v[:, h * W : (h + 1) * W]
-    row = lax.broadcasted_iota(jnp.int32, (8, W), 0)
-    first = gamma * kh[0:1]
+def make_masks(slots, heads, extra):
+    block = 4 * heads
+    shape = (slots * block + extra, slots * heads * W)
+    row = lax.broadcasted_iota(jnp.int32, shape, 0)
+    lane = lax.broadcasted_iota(jnp.int32, shape, 1)
+    return row % 4, (row // 4) == (lane // W), row
+
+
+def factors(keys, values, gamma, masks, queries=None):
+    term, own, row = masks
+    slots, heads = len(keys), keys[0].shape[1] // W
+    key = jnp.concatenate(keys, axis=1)
+    first = gamma * key[0:1]
     hi = first.astype(jnp.bfloat16).astype(jnp.float32)
     mid = (first - hi).astype(jnp.bfloat16).astype(jnp.float32)
     low = first - hi - mid
-    left = jnp.where(row == 0, hi, jnp.where(row == 1, mid, jnp.where(row == 2, low, jnp.where(row == 3, kh[1:2], 0.0))))
-    right = jnp.where(row < 3, vh[0:1], jnp.where(row == 3, vh[1:2], 0.0))
+    left = jnp.where(term == 0, hi, jnp.where(term == 1, mid, jnp.where(term == 2, low, key[1:2])))
+    left = jnp.where(own, left, 0.0)
+    line = lax.broadcasted_iota(jnp.int32, (row.shape[0], W), 0)
+    right = jnp.zeros((row.shape[0], W), jnp.float32)
+    for s in range(slots):
+        for h in range(heads):
+            at = 4 * (s * heads + h)
+            part = values[s][:, h * W : (h + 1) * W]
+            right = jnp.where((line >= at) & (line < at + 3), part[0:1], right)
+            right = jnp.where(line == at + 3, part[1:2], right)
+    if queries is not None:
+        at = 4 * slots * heads
+        query = jnp.concatenate(queries, axis=1)
+        left = jnp.where(row == at, query[0:1], jnp.where(row == at + 1, query[1:2], left))
+        ones = [jnp.where(line == at + t, 1.0, 0.0) for t in range(STEPS)]
+        right = jnp.concatenate([right, *ones], axis=1)
     return left, right
+
+
+def gamma_row(table_ref, index_ref, slots, heads):
+    lane = lax.broadcasted_iota(jnp.int32, (1, slots * heads * W), 1)
+    out = jnp.zeros(lane.shape, jnp.float32)
+    for h in range(heads):
+        out = jnp.where((lane // W) % heads == h, decay(table_ref, index_ref, h), out)
+    return out
 
 
 def outer(left, right):
@@ -102,23 +133,31 @@
         part = pl.ds(n * CAP, CAP)
         return pltpu.make_async_copy(buf_ref.at[part], out_any.at[part], out_sem.at[n])
 
+    masks = make_masks(CAP, heads, 0)
+    gamma = gamma_row(table_ref, index_ref, CAP, heads)
+
     def fill(n, carry):
+        slots, keys, values, keeps = [], [], [], []
         for position in range(CAP):
             found = map_ref[n * CAP + position]
             slot = jnp.maximum(found, 0)
-            on = jnp.where(active_ref[slot] > 0, 1.0, 0.0)
+            on = active_ref[slot] > 0
+            here = jnp.where(found >= 0, 1.0, 0.0)
             tokens = tok_ref[slot].astype(jnp.float32)
+            slots.append(slot)
+            keys.append(tokens[1] * jnp.where(on, here, 0.0))
+            values.append(tokens[2])
+            keeps.append([here * jnp.where(on, decay(table_ref, index_ref, h) ** 2, 1.0) for h in range(heads)])
+        added = outer(*factors(keys, values, gamma, masks))
+        for position in range(CAP):
             for h in range(heads):
-                gamma = decay(table_ref, index_ref, h)
-                left, right = rows_of(tokens[1], tokens[2], gamma, h)
-                keep = jnp.where(on > 0.0, gamma * gamma, 1.0)
-                final = keep * state_ref[slot, h] + outer(left * on, right)
-                final = jnp.where(found >= 0, final, 0.0)
+                at = (position * heads + h) * W
+                final = keeps[position][h] * state_ref[slots[position], h] + added[at : at + W]
                 buf_ref[n * CAP + position, h] = final.astype(jnp.bfloat16)
         store_of(n).start()
         return carry
 
-    lax.fori_loop(0, groups, fill, 0, unroll=2)
+    lax.fori_loop(0, groups, fill, 0, unroll=groups)
     for n in range(groups):
         store_of(n).wait()
 
@@ -129,12 +168,12 @@
     active_any,
     slot_any,
     dest_any,
-    tok_ref,
-    state_ref,
+    tok_any,
+    state_any,
     weight_any,
     after_any,
-    new_ref,
-    part0_any,
+    new_any,
+    part0_ref,
     part1_any,
     part2_any,
     part3_any,
@@ -143,6 +182,9 @@
     active_ref,
     slot_ref,
     dest_ref,
+    tok_ref,
+    state_ref,
+    new_ref,
     gone_ref,
     heads_ref,
     weight_ref,
@@ -150,87 +192,92 @@
     scalar_sem,
     weight_sem,
     parts_sem,
+    state_sem,
+    new_sem,
 ):
-    parts_any = (part0_any, part1_any, part2_any, part3_any)
+    parts_any = (part0_ref, part1_any, part2_any, part3_any)
     me = lax.axis_index("batch")
     entries = slot_ref.shape[1]
     heads = state_ref.shape[1]
-    batch = state_ref.shape[0]
-    i = pl.program_id(0)
+    count = state_ref.shape[0]
+    pairs = (
+        (table_any, table_ref),
+        (index_any, index_ref),
+        (active_any, active_ref),
+        (slot_any, slot_ref),
+        (dest_any, dest_ref),
+        (tok_any, tok_ref),
+    )
+    copies = [pltpu.make_async_copy(a, b, scalar_sem.at[n]) for n, (a, b) in enumerate(pairs)]
+    for copy in copies:
+        copy.start()
+    loads, stores = [], []
+    for n in range(count // PAIR):
+        part = pl.ds(n * PAIR, PAIR)
+        loads.append(pltpu.make_async_copy(state_any.at[part], state_ref.at[part], state_sem.at[n]))
+        stores.append(pltpu.make_async_copy(new_ref.at[part], new_any.at[part], new_sem.at[n]))
+        loads[n].start()
     load = pltpu.make_async_copy(weight_any, weight_ref, weight_sem)
-
-    @pl.when(i == 0)
-    def _():
-        pairs = (
-            (table_any, table_ref),
-            (index_any, index_ref),
-            (active_any, active_ref),
-            (slot_any, slot_ref),
-            (dest_any, dest_ref),
-        )
-        copies = [pltpu.make_async_copy(a, b, scalar_sem.at[n]) for n, (a, b) in enumerate(pairs)]
-        for copy in copies:
-            copy.start()
-        load.start()
-        for copy in copies:
-            copy.wait()
-        for s in range(gone_ref.shape[0]):
-            gone_ref[s] = 0
-        for j in range(entries):
-            slot = slot_ref[0, j]
-            moves = jnp.where(dest_ref[0, j] != me, 1, 0)
-            gone_ref[slot] = gone_ref[slot] + moves
+    load.start()
+    for copy in copies:
+        copy.wait()
+    for s in range(count):
+        gone_ref[s] = 0
+    for j in range(entries):
+        slot = slot_ref[0, j]
+        gone_ref[slot] = gone_ref[slot] + jnp.where(dest_ref[0, j] != me, 1, 0)
 
     row = lax.broadcasted_iota(jnp.int32, (8, W), 0)
-    wide = lax.broadcasted_iota(jnp.int32, (8, 2 * W), 0)
-    lane = lax.broadcasted_iota(jnp.int32, (8, 2 * W), 1)
-    ones = jnp.where((wide == 4) & (lane < W), 1.0, jnp.where((wide == 5) & (lane >= W), 1.0, 0.0))
-    for b in range(batch):
-        r = i * batch + b
-        on = active_ref[r] > 0
-        gone = gone_ref[r] > 0
-        tokens = tok_ref[b].astype(jnp.float32)
-        query, key, value = tokens[0], tokens[1], tokens[2]
-        for h in range(heads):
-            part = slice(h * W, (h + 1) * W)
-            q, k, v = query[:, part], key[:, part], value[:, part]
-            gamma = decay(table_ref, index_ref, h)
-            left, right = rows_of(key, value, gamma, h)
-            left = jnp.where(row == 4, q[0:1], jnp.where(row == 5, q[1:2], left))
-            mixed = outer(left, jnp.concatenate([right, ones], axis=1))
-            before = state_ref[b, h]
-            raw1 = gamma * jnp.sum(mixed[:, W : 2 * W] * before, axis=0, keepdims=True)
-            raw1 = raw1 + jnp.sum(q[0:1] * k[0:1], axis=1, keepdims=True) * v[0:1]
-            final = (gamma * gamma) * before + mixed[:, :W]
-            raw2 = jnp.sum(mixed[:, 2 * W :] * final, axis=0, keepdims=True)
-            raw = jnp.where(row == 0, raw1, jnp.where(row == 1, raw2, 0.0))
-            scaled = raw * lax.rsqrt(jnp.mean(raw * raw, axis=1, keepdims=True) + 1e-06)
-            heads_ref[r, :, part] = jnp.where(on, scaled, 0.0)
-            final = jnp.where(on, final, before)
-            new_ref[b, h] = jnp.where(gone, 0.0, final)
-
-    @pl.when(i == pl.num_programs(0) - 1)
-    def _():
-        count, padded, depth = heads_ref.shape
-        rows = count * STEPS
-        line = lax.broadcasted_iota(jnp.int32, (rows, count * padded), 0)
-        source = lax.broadcasted_iota(jnp.int32, (rows, count * padded), 1)
-        pick = jnp.where(source == (line // STEPS) * padded + line % STEPS, 1.0, 0.0).astype(jnp.bfloat16)
-        out = heads_ref[...].reshape(count * padded, depth).astype(jnp.bfloat16)
-        out = jnp.dot(pick, out, preferred_element_type=jnp.float32).astype(jnp.bfloat16)
-        load.wait()
-        share = parts_ref.shape[3]
-        column = lax.axis_index("tensor")
-        stores = []
-        for dx in (1, 2, 3, 0):
-            for dy in range(SIDE):
-                block = lax.rem(column // SIDE + dx, SIDE) * SIDE + lax.rem(column + dy, SIDE)
-                weight = weight_ref[:, pl.ds(pl.multiple_of(block * share, share), share)]
-                parts_ref[dx, dy] = jnp.dot(out, weight, preferred_element_type=jnp.float32)
-            stores.append(pltpu.make_async_copy(parts_ref.at[dx], parts_any[dx], parts_sem.at[dx]))
-            stores[-1].start()
-        for store in stores:
-            store.wait()
+    masks = make_masks(PAIR, heads, 16)
+    gammas = gamma_row(table_ref, index_ref, PAIR, heads)
+    for part in loads:
+        part.wait()
+    for pair in range(count // PAIR):
+        at = [pair * PAIR + n for n in range(PAIR)]
+        tokens = [tok_ref[b].astype(jnp.float32) for b in at]
+        on = [active_ref[b] > 0 for b in at]
+        live = [jnp.where(gone_ref[b] > 0, 0.0, 1.0) for b in at]
+        keys = [token[1] * jnp.where(flag, 1.0, 0.0) for token, flag in zip(tokens, on)]
+        mixed = outer(*factors(keys, [token[2] for token in tokens], gammas, masks, [token[0] for token in tokens]))
+        for n, b in enumerate(at):
+            for h in range(heads):
+                part = slice(h * W, (h + 1) * W)
+                q, k, v = tokens[n][0][:, part], keys[n][:, part], tokens[n][2][:, part]
+                gamma = decay(table_ref, index_ref, h)
+                top = (n * heads + h) * W
+                before = state_ref[b, h]
+                raw1 = gamma * jnp.sum(mixed[top : top + W, W : 2 * W] * before, axis=0, keepdims=True)
+                raw1 = raw1 + jnp.sum(q[0:1] * k[0:1], axis=1, keepdims=True) * v[0:1]
+                final = jnp.where(on[n], gamma * gamma, 1.0) * before + mixed[top : top + W, :W]
+                raw2 = jnp.sum(mixed[top : top + W, 2 * W :] * final, axis=0, keepdims=True)
+                raw = jnp.where(row == 0, raw1, jnp.where(row == 1, raw2, 0.0))
+                scaled = raw * lax.rsqrt(jnp.mean(raw * raw, axis=1, keepdims=True) + 1e-06)
+                heads_ref[b, :, part] = jnp.where(on[n], scaled, 0.0)
+                new_ref[b, h] = live[n] * final
+        stores[pair].start()
+
+    count, padded, depth = heads_ref.shape
+    rows = count * STEPS
+    line = lax.broadcasted_iota(jnp.int32, (rows, count * padded), 0)
+    source = lax.broadcasted_iota(jnp.int32, (rows, count * padded), 1)
+    pick = jnp.where(source == (line // STEPS) * padded + line % STEPS, 1.0, 0.0).astype(jnp.bfloat16)
+    out = heads_ref[...].reshape(count * padded, depth).astype(jnp.bfloat16)
+    out = jnp.dot(pick, out, preferred_element_type=jnp.float32).astype(jnp.bfloat16)
+    load.wait()
+    share = parts_ref.shape[3]
+    column = lax.axis_index("tensor")
+    sends = []
+    for dx in (1, 2, 3, 0):
+        for dy in range(SIDE):
+            block = lax.rem(column // SIDE + dx, SIDE) * SIDE + lax.rem(column + dy, SIDE)
+            weight = weight_ref[:, pl.ds(pl.multiple_of(block * share, share), share)]
+            target = parts_ref.at[dx - 1, dy] if dx else part0_ref.at[dy]
+            target[...] = jnp.dot(out, weight, preferred_element_type=jnp.float32)
+        if dx:
+            sends.append(pltpu.make_async_copy(parts_ref.at[dx - 1], parts_any[dx], parts_sem.at[dx - 1]))
+            sends[-1].start()
+    for store in [*stores, *sends]:
+        store.wait()
 
 
 def add_kernel(a_ref, b_ref, c_ref, d_ref, *out_refs):
@@ -256,17 +303,13 @@
         residual_ref[r] = hsum[part].astype(jnp.bfloat16)
 
 
-def widen_kernel(landed_any, arrived_any, in_ref, wide_ref, in_sem, out_sem):
-    chunks, size = in_ref.shape[:2]
-    loads, stores = [], []
+def widen_kernel(landed_ref, arrived_any, wide_ref, out_sem):
+    chunks, size = wide_ref.shape[:2]
+    stores = []
     for n in range(chunks):
         part = pl.ds(n * size, size)
-        loads.append(pltpu.make_async_copy(landed_any.at[part], in_ref.at[n], in_sem.at[n]))
-        loads[n].start()
+        wide_ref[n] = landed_ref[part].astype(jnp.float32)
         stores.append(pltpu.make_async_copy(wide_ref.at[n], arrived_any.at[part], out_sem.at[n]))
-    for n in range(chunks):
-        loads[n].wait()
-        wide_ref[n] = in_ref[n].astype(jnp.float32)
         stores[n].start()
     for store in stores:
         store.wait()
@@ -342,31 +385,29 @@
     )(*(here(value) for value in (*scalars, tokens, state)))
     landed = lax.all_to_all(leaving, "batch", split_axis=0, concat_axis=0, tiled=True)
 
-    grid = 4
     new_state, *parts = pl.pallas_call(
         decode_kernel,
-        grid=(grid,),
         out_shape=(
             pltpu.HBM(state.shape, f32),
-            *[pltpu.HBM((SIDE, rows, share), f32)] * SIDE,
+            jax.ShapeDtypeStruct((SIDE, rows, share), f32),
+            *[pltpu.HBM((SIDE, rows, share), f32)] * (SIDE - 1),
         ),
-        in_specs=[HBM] * 5
-        + [
-            pl.BlockSpec((count // grid, 3, STEPS, heads * width), lambda i: (i, 0, 0, 0)),
-            pl.BlockSpec((count // grid, heads, width, width), lambda i: (i, 0, 0, 0)),
-            HBM,
-            HBM,
-        ],
-        out_specs=(pl.BlockSpec((count // grid, heads, width, width), lambda i: (i, 0, 0, 0)), *[HBM] * SIDE),
+        in_specs=[HBM] * 9,
+        out_specs=[HBM, VMEM] + [HBM] * (SIDE - 1),
         scratch_shapes=[
             *scalar_scratch,
+            pltpu.VMEM(tokens.shape, bf16),
+            pltpu.VMEM(state.shape, f32),
+            pltpu.VMEM(state.shape, f32),
             pltpu.SMEM((count,), jnp.int32),
             pltpu.VMEM((count, 8, heads * width), f32),
             pltpu.VMEM(out_weight.shape, bf16),
-            pltpu.VMEM((SIDE, SIDE, rows, share), f32),
-            dma((5,)),
+            pltpu.VMEM((SIDE - 1, SIDE, rows, share), f32),
+            dma((6,)),
             dma,
-            dma((SIDE,)),
+            dma((SIDE - 1,)),
+            dma((count // PAIR,)),
+            dma((count // PAIR,)),
         ],
         compiler_params=params(),
         cost_estimate=pl.CostEstimate(flops=32 * 20 * width * width, bytes_accessed=8 << 20, transcendentals=0),
@@ -405,14 +446,9 @@
     arrived = pl.pallas_call(
         widen_kernel,
         out_shape=pltpu.HBM(moved, f32),
-        in_specs=[pl.BlockSpec(memory_space=pl.ANY)],
+        in_specs=[VMEM],
         out_specs=HBM,
-        scratch_shapes=[
-            pltpu.VMEM((chunks, moved[0] // chunks) + pair[1:], bf16),
-            pltpu.VMEM((chunks, moved[0] // chunks) + pair[1:], f32),
-            dma((chunks,)),
-            dma((chunks,)),
-        ],
+        scratch_shapes=[pltpu.VMEM((chunks, moved[0] // chunks) + pair[1:], f32), dma((chunks,))],
         compiler_params=params(),
         name="widen",
     )(landed)

time: 66.9 us -> 65.3 us (0.976)
  Pallas kernels: 15.4 us -> 10.9 us
  waiting for transfers between devices: 22.1 us -> 26 us
  local copies, waits for them, and re-layouts: 0.97 us -> 0.01 us
    all_to_all x1, waiting for transfers between devices: 3.15 us -> 7.04 us  [body(): lax.all_to_all(leaving, 'batch', split_axis=0, concat_axis=0, tiled=True)]
    pallas_call x2, Pallas kernels: 9.75 us -> 6.6 us  [the longest x1 4.5 us: body(): pl.pallas_call(decode_kernel, out_shape=(pltpu.HBM(state.shape, f32), jax...]
    pallas_call x1, Pallas kernels: 4.76 us -> 3.39 us  [body(): pl.pallas_call(leave_kernel, out_shape=pltpu.HBM(moved, bf16), in_specs=[...]
    unnamed x6 -> x4, local copies, waits for them, and re-layouts: 0.96 us -> 0.01 us
  transfers between devices with their start and end apart: 13 -> 13, of which waited for: 10 -> 10; matrix products, arithmetic and copies ran while one was open for 0% -> 0% of each run, Pallas kernels for 12% -> 8%
where the time goes in v3:
time: 65.3 us; the launch traced here: 65.1 us
  starting transfers between devices  27.5 us (42%)
  waiting for transfers between devices  26 us (40%)
  Pallas kernels  10.9 us (17%)
  between operations  0.68 us (1%)
    ppermute x6, waiting for transfers between devices, shift_x(): lax.ppermute(value, 'tensor', [(x * SIDE + y, (x + d) % SIDE * SIDE + y)...  12.9 us
    all_to_all x1, starting transfers between devices, body(): lax.all_to_all(leaving, 'batch', split_axis=0, concat_axis=0, tiled=True)  9.99 us
    ppermute x6, starting transfers between devices, shift_x(): lax.ppermute(value, 'tensor', [(x * SIDE + y, (x + d) % SIDE * SIDE + y)...  9.37 us
    ppermute x6, starting transfers between devices, shift_y(): lax.ppermute(value, 'tensor', [(x * SIDE + y, x * SIDE + (y + d) % SIDE)...  8.15 us
    all_to_all x1, waiting for transfers between devices, body(): lax.all_to_all(leaving, 'batch', split_axis=0, concat_axis=0, tiled=True)  7.04 us
    ppermute x6, waiting for transfers between devices, shift_y(): lax.ppermute(value, 'tensor', [(x * SIDE + y, x * SIDE + (y + d) % SIDE)...  6.1 us
    pallas_call x1, Pallas kernels, body(): pl.pallas_call(decode_kernel, out_shape=(pltpu.HBM(state.shape, f32), jax...  4.5 us
    pallas_call x1, Pallas kernels, body(): pl.pallas_call(leave_kernel, out_shape=pltpu.HBM(moved, bf16), in_specs=[...  3.39 us
  transfers between devices with their start and end apart: 13, of which 10 were waited for; matrix products, arithmetic and copies ran while one was open for 0% of the time, Pallas kernels for 8%

profile of v3, /device:TPU:1, one launch (start us, length us, event | category | flops | bytes accessed | tf_op | source)
XLA Modules:
  0.0 65.1 jit_solution(13519813504974230167)
XLA Ops:
  0.6 3.4 %leave.1.after_any = bf16[32,2,128,128]{3,2,1,0:T(8,128)(2,1)} custom-call(f32[16]{0:T(128)} %table_any.3, s32[2]{0:T(128)} %index_any.3, s32[16]{0:T(128)} %active_any.3, s32[1,16]{1,0:T(1,128)} %slot_any.3, s32[1,16]{1,0:T(1,128)} %dest_any.3, bf16[16,3,2,256]{3,2,1,0:T(2,128)(2,1)} %bitcast.1, f32[16,2,128,128]{3,2,1,0:T(8,128)} %state_any.3), custom_call_target="tpu_custom_call" | custom-call | flops 10485760 | bytes 8388608 | tf_op jit(solution)/shard_map/leave/pallas_call | solution.py:368
  4.0 10.0 %all-to-all-start = ((bf16[32,2,128,128]{3,2,1,0:T(8,128)(2,1)}), bf16[32,2,128,128]{3,2,1,0:T(8,128)(2,1)S(1)}, u32[]{:S(2)}, u32[]{:S(2)}) async-start(bf16[32,2,128,128]{3,2,1,0:T(8,128)(2,1)} %leave.1.after_any), calls=%async_computation | async-start | bytes 4194304 | tf_op jit(solution)/shard_map/all_to_all | solution.py:386
  14.0 4.5 %decode.1 = (f32[16,2,128,128]{3,2,1,0:T(8,128)}, f32[4,32,512]{2,1,0:T(8,128)S(1)}, f32[4,32,512]{2,1,0:T(8,128)}, f32[4,32,512]{2,1,0:T(8,128)}, f32[4,32,512]{2,1,0:T(8,128)}) custom-call(f32[16]{0:T(128)} %table_any.3, s32[2]{0:T(128)} %index_any.3, s32[16]{0:T(128)} %active_any.3, s32[1,16]{1,0:T(1,128)} %slot_any.3, s32[1,16]{1,0:T(1,128)} %dest_any.3, ...), custom_call_target="tpu_custom_call" | custom-call | flops 10485760 | bytes 8388608 | tf_op jit(solution)/shard_map/decode/pallas_call | solution.py:388
  18.5 1.3 %collective-permute-start = (f32[4,32,512]{2,1,0:T(8,128)}, f32[4,32,512]{2,1,0:T(8,128)S(1)}, u32[]{:S(2)}, u32[]{:S(2)}) collective-permute-start(f32[4,32,512]{2,1,0:T(8,128)} %get-tuple-element.18), channel_id=1, source_target_pairs={{0,4},{1,5},{2,6},{3,7},{4,8},{5,9},{6,10},{7,11},{8,12},{9,13},{1... | collective-permute-start | bytes 786440 | tf_op jit(solution)/shard_map/ppermute | solution.py:319
  19.9 2.5 %collective-permute-start.1 = (f32[4,32,512]{2,1,0:T(8,128)}, f32[4,32,512]{2,1,0:T(8,128)S(1)}, u32[]{:S(2)}, u32[]{:S(2)}) collective-permute-start(f32[4,32,512]{2,1,0:T(8,128)} %get-tuple-element.19), channel_id=1, source_target_pairs={{0,8},{1,9},{2,10},{3,11},{4,12},{5,13},{6,14},{7,15},{8,0},{9,1},... | collective-permute-start | bytes 786440 | tf_op jit(solution)/shard_map/ppermute | solution.py:319
  22.3 1.2 %collective-permute-start.2 = (f32[4,32,512]{2,1,0:T(8,128)}, f32[4,32,512]{2,1,0:T(8,128)S(1)}, u32[]{:S(2)}, u32[]{:S(2)}) collective-permute-start(f32[4,32,512]{2,1,0:T(8,128)} %get-tuple-element.20), channel_id=1, source_target_pairs={{0,12},{1,13},{2,14},{3,15},{4,0},{5,1},{6,2},{7,3},{8,4},{9,5},{1... | collective-permute-start | bytes 786440 | tf_op jit(solution)/shard_map/ppermute | solution.py:319
  23.5 4.5 %collective-permute-done.b_ref = f32[4,32,512]{2,1,0:T(8,128)S(1)} collective-permute-done((f32[4,32,512]{2,1,0:T(8,128)}, f32[4,32,512]{2,1,0:T(8,128)S(1)}, u32[]{:S(2)}, u32[]{:S(2)}) %collective-permute-start) | collective-permute-done | bytes 262176 | tf_op jit(solution)/shard_map/ppermute | solution.py:319
  27.9 6.6 %collective-permute-done.1.c_ref = f32[4,32,512]{2,1,0:T(8,128)S(1)} collective-permute-done((f32[4,32,512]{2,1,0:T(8,128)}, f32[4,32,512]{2,1,0:T(8,128)S(1)}, u32[]{:S(2)}, u32[]{:S(2)}) %collective-permute-start.1) | collective-permute-done | bytes 262176 | tf_op jit(solution)/shard_map/ppermute | solution.py:319
  34.6 1.4 %collective-permute-start.3 = (f32[32,512]{1,0:T(8,128)S(1)}, f32[32,512]{1,0:T(8,128)S(1)}, u32[]{:S(2)}, u32[]{:S(2)}) collective-permute-start(f32[32,512]{1,0:T(8,128)S(1)} %get-tuple-element.22), channel_id=1, source_target_pairs={{0,1},{1,2},{2,3},{3,0},{4,5},{5,6},{6,7},{7,4},{8,9},{9,10},{10,1... | collective-permute-start | bytes 196616 | tf_op jit(solution)/shard_map/ppermute | solution.py:325
  36.0 2.6 %collective-permute-start.4 = (f32[32,512]{1,0:T(8,128)S(1)}, f32[32,512]{1,0:T(8,128)S(1)}, u32[]{:S(2)}, u32[]{:S(2)}) collective-permute-start(f32[32,512]{1,0:T(8,128)S(1)} %get-tuple-element.23), channel_id=1, source_target_pairs={{0,2},{1,3},{2,0},{3,1},{4,6},{5,7},{6,4},{7,5},{8,10},{9,11},{10,... | collective-permute-start | bytes 196616 | tf_op jit(solution)/shard_map/ppermute | solution.py:325
  38.6 1.1 %collective-permute-start.5 = (f32[32,512]{1,0:T(8,128)S(1)}, f32[32,512]{1,0:T(8,128)S(1)}, u32[]{:S(2)}, u32[]{:S(2)}) collective-permute-start(f32[32,512]{1,0:T(8,128)S(1)} %get-tuple-element.24), channel_id=1, source_target_pairs={{0,3},{1,0},{2,1},{3,2},{4,7},{5,4},{6,5},{7,6},{8,11},{9,8},{10,9... | collective-permute-start | bytes 196616 | tf_op jit(solution)/shard_map/ppermute | solution.py:325
  39.6 1.6 %collective-permute-done.4.c_ref = f32[32,512]{1,0:T(8,128)S(1)} collective-permute-done((f32[32,512]{1,0:T(8,128)S(1)}, f32[32,512]{1,0:T(8,128)S(1)}, u32[]{:S(2)}, u32[]{:S(2)}) %collective-permute-start.4) | collective-permute-done | bytes 65568 | tf_op jit(solution)/shard_map/ppermute | solution.py:325
  41.3 0.9 %collective-permute-done.5.d_ref = f32[32,512]{1,0:T(8,128)S(1)} collective-permute-done((f32[32,512]{1,0:T(8,128)S(1)}, f32[32,512]{1,0:T(8,128)S(1)}, u32[]{:S(2)}, u32[]{:S(2)}) %collective-permute-start.5) | collective-permute-done | bytes 65568 | tf_op jit(solution)/shard_map/ppermute | solution.py:325
  42.3 1.1 %collective-permute-start.6 = (f32[32,128]{1,0:T(8,128)S(1)}, f32[32,128]{1,0:T(8,128)S(1)}, u32[]{:S(2)}, u32[]{:S(2)}) collective-permute-start(f32[32,128]{1,0:T(8,128)S(1)} %get-tuple-element.26), channel_id=1, source_target_pairs={{0,4},{1,5},{2,6},{3,7},{4,8},{5,9},{6,10},{7,11},{8,12},{9,13},{1... | collective-permute-start | bytes 49160 | tf_op jit(solution)/shard_map/ppermute | solution.py:319
  43.4 2.3 %collective-permute-start.7 = (f32[32,128]{1,0:T(8,128)S(1)}, f32[32,128]{1,0:T(8,128)S(1)}, u32[]{:S(2)}, u32[]{:S(2)}) collective-permute-start(f32[32,128]{1,0:T(8,128)S(1)} %get-tuple-element.26), channel_id=1, source_target_pairs={{0,8},{1,9},{2,10},{3,11},{4,12},{5,13},{6,14},{7,15},{8,0},{9,1},... | collective-permute-start | bytes 49160 | tf_op jit(solution)/shard_map/ppermute | solution.py:319
  45.7 1.1 %collective-permute-start.8 = (f32[32,128]{1,0:T(8,128)S(1)}, f32[32,128]{1,0:T(8,128)S(1)}, u32[]{:S(2)}, u32[]{:S(2)}) collective-permute-start(f32[32,128]{1,0:T(8,128)S(1)} %get-tuple-element.26), channel_id=1, source_target_pairs={{0,12},{1,13},{2,14},{3,15},{4,0},{5,1},{6,2},{7,3},{8,4},{9,5},{1... | collective-permute-start | bytes 49160 | tf_op jit(solution)/shard_map/ppermute | solution.py:319
  46.8 1.0 %collective-permute-done.7 = f32[32,128]{1,0:T(8,128)S(1)} collective-permute-done((f32[32,128]{1,0:T(8,128)S(1)}, f32[32,128]{1,0:T(8,128)S(1)}, u32[]{:S(2)}, u32[]{:S(2)}) %collective-permute-start.7) | collective-permute-done | bytes 16416 | tf_op jit(solution)/shard_map/ppermute | solution.py:319
  47.7 0.8 %collective-permute-done.8 = f32[32,128]{1,0:T(8,128)S(1)} collective-permute-done((f32[32,128]{1,0:T(8,128)S(1)}, f32[32,128]{1,0:T(8,128)S(1)}, u32[]{:S(2)}, u32[]{:S(2)}) %collective-permute-start.8) | collective-permute-done | bytes 16416 | tf_op jit(solution)/shard_map/ppermute | solution.py:319
  48.6 1.6 %collective-permute-start.10 = (f32[32,128]{1,0:T(8,128)S(1)}, f32[32,128]{1,0:T(8,128)S(1)}, u32[]{:S(2)}, u32[]{:S(2)}) collective-permute-start(f32[32,128]{1,0:T(8,128)S(1)} %add_add_fusion.a_ref), channel_id=1, source_target_pairs={{0,2},{1,3},{2,0},{3,1},{4,6},{5,7},{6,4},{7,5},{8,10},{9,11},{10,... | collective-permute-start | bytes 49160 | tf_op jit(solution)/shard_map/ppermute | solution.py:325
  50.2 1.0 %collective-permute-start.11 = (f32[32,128]{1,0:T(8,128)S(1)}, f32[32,128]{1,0:T(8,128)S(1)}, u32[]{:S(2)}, u32[]{:S(2)}) collective-permute-start(f32[32,128]{1,0:T(8,128)S(1)} %add_add_fusion.a_ref), channel_id=1, source_target_pairs={{0,3},{1,0},{2,1},{3,2},{4,7},{5,4},{6,5},{7,6},{8,11},{9,8},{10,9... | collective-permute-start | bytes 49160 | tf_op jit(solution)/shard_map/ppermute | solution.py:325
  51.7 1.3 %collective-permute-done.10.c_ref = f32[32,128]{1,0:T(8,128)S(1)} collective-permute-done((f32[32,128]{1,0:T(8,128)S(1)}, f32[32,128]{1,0:T(8,128)S(1)}, u32[]{:S(2)}, u32[]{:S(2)}) %collective-permute-start.10) | collective-permute-done | bytes 16416 | tf_op jit(solution)/shard_map/ppermute | solution.py:325
  53.1 2.2 %collective-permute-done.9.b_ref = f32[32,128]{1,0:T(8,128)S(1)} collective-permute-done((f32[32,128]{1,0:T(8,128)S(1)}, f32[32,128]{1,0:T(8,128)S(1)}, u32[]{:S(2)}, u32[]{:S(2)}) %collective-permute-start.9) | collective-permute-done | bytes 16416 | tf_op jit(solution)/shard_map/ppermute | solution.py:325
  55.9 7.0 %all-to-all-done.landed_ref = bf16[32,2,128,128]{3,2,1,0:T(8,128)(2,1)S(1)} async-done(((bf16[32,2,128,128]{3,2,1,0:T(8,128)(2,1)}), bf16[32,2,128,128]{3,2,1,0:T(8,128)(2,1)S(1)}, u32[]{:S(2)}, u32[]{:S(2)}) %all-to-all-start) | async-done | bytes 2097184 | tf_op jit(solution)/shard_map/all_to_all | solution.py:386
  63.0 2.1 %widen.1 = f32[32,2,128,128]{3,2,1,0:T(8,128)} custom-call(bf16[32,2,128,128]{3,2,1,0:T(8,128)(2,1)S(1)} %all-to-all-done.landed_ref), custom_call_target="tpu_custom_call" | custom-call | tf_op jit(solution)/shard_map/widen/pallas_call | solution.py:446
  (14 shorter events, 1.5 us)
Async XLA Ops:
  4.0 58.9 %all-to-all-start = ((bf16[32,2,128,128]{3,2,1,0:T(8,128)(2,1)}), bf16[32,2,128,128]{3,2,1,0:T(8,128)(2,1)S(1)}, u32[]{:S(2)}, u32[]{:S(2)}) async-start(bf16[32,2,128,128]{3,2,1,0:T(8,128)(2,1)} %leave.1.after_any), calls=%async_computation | async-start | bytes 4194304 | tf_op jit(solution)/shard_map/all_to_all | solution.py:386
  14.0 28.2 %copy-start = (bf16[16,2,512]{2,1,0:T(2,128)(2,1)S(1)}, bf16[16,2,512]{2,1,0:T(2,128)(2,1)}, u32[]{:S(2)}) copy-start(bf16[16,2,512]{2,1,0:T(2,128)(2,1)} %residual_ref.1) | copy-start | bytes 98308
  14.0 37.6 %copy-start.1 = (bf16[512]{0:T(512)(128)(2,1)S(1)}, bf16[512]{0:T(512)(128)(2,1)}, u32[]{:S(2)}) copy-start(bf16[512]{0:T(512)(128)(2,1)} %param.18) | copy-start | bytes 3076
  18.5 9.4 %collective-permute-start = (f32[4,32,512]{2,1,0:T(8,128)}, f32[4,32,512]{2,1,0:T(8,128)S(1)}, u32[]{:S(2)}, u32[]{:S(2)}) collective-permute-start(f32[4,32,512]{2,1,0:T(8,128)} %get-tuple-element.18), channel_id=1, source_target_pairs={{0,4},{1,5},{2,6},{3,7},{4,8},{5,9},{6,10},{7,11},{8,12},{9,13},{1... | collective-permute-start | bytes 786440 | tf_op jit(solution)/shard_map/ppermute | solution.py:319
  19.9 14.7 %collective-permute-start.1 = (f32[4,32,512]{2,1,0:T(8,128)}, f32[4,32,512]{2,1,0:T(8,128)S(1)}, u32[]{:S(2)}, u32[]{:S(2)}) collective-permute-start(f32[4,32,512]{2,1,0:T(8,128)} %get-tuple-element.19), channel_id=1, source_target_pairs={{0,8},{1,9},{2,10},{3,11},{4,12},{5,13},{6,14},{7,15},{8,0},{9,1},... | collective-permute-start | bytes 786440 | tf_op jit(solution)/shard_map/ppermute | solution.py:319
  22.3 12.2 %collective-permute-start.2 = (f32[4,32,512]{2,1,0:T(8,128)}, f32[4,32,512]{2,1,0:T(8,128)S(1)}, u32[]{:S(2)}, u32[]{:S(2)}) collective-permute-start(f32[4,32,512]{2,1,0:T(8,128)} %get-tuple-element.20), channel_id=1, source_target_pairs={{0,12},{1,13},{2,14},{3,15},{4,0},{5,1},{6,2},{7,3},{8,4},{9,5},{1... | collective-permute-start | bytes 786440 | tf_op jit(solution)/shard_map/ppermute | solution.py:319
  34.6 5.1 %collective-permute-start.3 = (f32[32,512]{1,0:T(8,128)S(1)}, f32[32,512]{1,0:T(8,128)S(1)}, u32[]{:S(2)}, u32[]{:S(2)}) collective-permute-start(f32[32,512]{1,0:T(8,128)S(1)} %get-tuple-element.22), channel_id=1, source_target_pairs={{0,1},{1,2},{2,3},{3,0},{4,5},{5,6},{6,7},{7,4},{8,9},{9,10},{10,1... | collective-permute-start | bytes 196616 | tf_op jit(solution)/shard_map/ppermute | solution.py:325
  36.0 5.3 %collective-permute-start.4 = (f32[32,512]{1,0:T(8,128)S(1)}, f32[32,512]{1,0:T(8,128)S(1)}, u32[]{:S(2)}, u32[]{:S(2)}) collective-permute-start(f32[32,512]{1,0:T(8,128)S(1)} %get-tuple-element.23), channel_id=1, source_target_pairs={{0,2},{1,3},{2,0},{3,1},{4,6},{5,7},{6,4},{7,5},{8,10},{9,11},{10,... | collective-permute-start | bytes 196616 | tf_op jit(solution)/shard_map/ppermute | solution.py:325
  38.6 3.6 %collective-permute-start.5 = (f32[32,512]{1,0:T(8,128)S(1)}, f32[32,512]{1,0:T(8,128)S(1)}, u32[]{:S(2)}, u32[]{:S(2)}) collective-permute-start(f32[32,512]{1,0:T(8,128)S(1)} %get-tuple-element.24), channel_id=1, source_target_pairs={{0,3},{1,0},{2,1},{3,2},{4,7},{5,4},{6,5},{7,6},{8,11},{9,8},{10,9... | collective-permute-start | bytes 196616 | tf_op jit(solution)/shard_map/ppermute | solution.py:325
  42.3 4.5 %collective-permute-start.6 = (f32[32,128]{1,0:T(8,128)S(1)}, f32[32,128]{1,0:T(8,128)S(1)}, u32[]{:S(2)}, u32[]{:S(2)}) collective-permute-start(f32[32,128]{1,0:T(8,128)S(1)} %get-tuple-element.26), channel_id=1, source_target_pairs={{0,4},{1,5},{2,6},{3,7},{4,8},{5,9},{6,10},{7,11},{8,12},{9,13},{1... | collective-permute-start | bytes 49160 | tf_op jit(solution)/shard_map/ppermute | solution.py:319
  43.4 4.4 %collective-permute-start.7 = (f32[32,128]{1,0:T(8,128)S(1)}, f32[32,128]{1,0:T(8,128)S(1)}, u32[]{:S(2)}, u32[]{:S(2)}) collective-permute-start(f32[32,128]{1,0:T(8,128)S(1)} %get-tuple-element.26), channel_id=1, source_target_pairs={{0,8},{1,9},{2,10},{3,11},{4,12},{5,13},{6,14},{7,15},{8,0},{9,1},... | collective-permute-start | bytes 49160 | tf_op jit(solution)/shard_map/ppermute | solution.py:319
  45.7 2.9 %collective-permute-start.8 = (f32[32,128]{1,0:T(8,128)S(1)}, f32[32,128]{1,0:T(8,128)S(1)}, u32[]{:S(2)}, u32[]{:S(2)}) collective-permute-start(f32[32,128]{1,0:T(8,128)S(1)} %get-tuple-element.26), channel_id=1, source_target_pairs={{0,12},{1,13},{2,14},{3,15},{4,0},{5,1},{6,2},{7,3},{8,4},{9,5},{1... | collective-permute-start | bytes 49160 | tf_op jit(solution)/shard_map/ppermute | solution.py:319
  48.6 4.4 %collective-permute-start.10 = (f32[32,128]{1,0:T(8,128)S(1)}, f32[32,128]{1,0:T(8,128)S(1)}, u32[]{:S(2)}, u32[]{:S(2)}) collective-permute-start(f32[32,128]{1,0:T(8,128)S(1)} %add_add_fusion.a_ref), channel_id=1, source_target_pairs={{0,2},{1,3},{2,0},{3,1},{4,6},{5,7},{6,4},{7,5},{8,10},{9,11},{10,... | collective-permute-start | bytes 49160 | tf_op jit(solution)/shard_map/ppermute | solution.py:325
  50.2 2.9 %collective-permute-start.11 = (f32[32,128]{1,0:T(8,128)S(1)}, f32[32,128]{1,0:T(8,128)S(1)}, u32[]{:S(2)}, u32[]{:S(2)}) collective-permute-start(f32[32,128]{1,0:T(8,128)S(1)} %add_add_fusion.a_ref), channel_id=1, source_target_pairs={{0,3},{1,0},{2,1},{3,2},{4,7},{5,4},{6,5},{7,6},{8,11},{9,8},{10,9... | collective-permute-start | bytes 49160 | tf_op jit(solution)/shard_map/ppermute | solution.py:325
  51.1 4.1 %collective-permute-start.9 = (f32[32,128]{1,0:T(8,128)S(1)}, f32[32,128]{1,0:T(8,128)S(1)}, u32[]{:S(2)}, u32[]{:S(2)}) collective-permute-start(f32[32,128]{1,0:T(8,128)S(1)} %add_add_fusion.a_ref), channel_id=1, source_target_pairs={{0,1},{1,2},{2,3},{3,0},{4,5},{5,6},{6,7},{7,4},{8,9},{9,10},{10,1... | collective-permute-start | bytes 49160 | tf_op jit(solution)/shard_map/ppermute | solution.py:325

commit v4 on v3

--- a/solution.py
+++ b/solution.py
@@ -90,76 +90,74 @@
     tok_ref,
     state_ref,
     buf_ref,
-    map_ref,
+    row_ref,
     in_sem,
+    state_sem,
     out_sem,
 ):
     me = lax.axis_index("batch")
+    count, heads = state_ref.shape[:2]
     entries = slot_ref.shape[1]
-    heads = state_ref.shape[1]
-    groups = map_ref.shape[0] // CAP
+    spare = out_any.shape[0]
     pairs = (
-        (state_any, state_ref),
-        (tok_any, tok_ref),
         (slot_any, slot_ref),
         (dest_any, dest_ref),
         (active_any, active_ref),
         (table_any, table_ref),
         (index_any, index_ref),
-    )
-    loads = [pltpu.make_async_copy(a, b, in_sem.at[n]) for n, (a, b) in enumerate(pairs)]
+        (tok_any, tok_ref),
+    )
+    copies = [pltpu.make_async_copy(a, b, in_sem.at[n]) for n, (a, b) in enumerate(pairs)]
+    for copy in copies:
+        copy.start()
+    loads = []
+    for n in range(count // PAIR):
+        part = pl.ds(n * PAIR, PAIR)
+        loads.append(pltpu.make_async_copy(state_any.at[part], state_ref.at[part], state_sem.at[n]))
+        loads[n].start()
+    for n in range(spare):
+        row_ref[n] = count
+    buf_ref[count] = jnp.zeros(buf_ref.shape[1:], buf_ref.dtype)
+    for copy in copies:
+        copy.wait()
+    for j in range(entries):
+        dest = dest_ref[0, j]
+        position = jnp.where(row_ref[dest * CAP] < count, 1, 0)
+        row_ref[jnp.where(dest != me, dest * CAP + position, spare)] = slot_ref[0, j]
+
+    def store_of(n, slot):
+        return pltpu.make_async_copy(buf_ref.at[pl.ds(slot, 1)], out_any.at[pl.ds(n, 1)], out_sem.at[n])
+
+    for n in range(spare):
+
+        @pl.when(row_ref[n] >= count)
+        def _(n=n):
+            store_of(n, count).start()
+
+    masks = make_masks(PAIR, heads, 0)
+    gammas = gamma_row(table_ref, index_ref, PAIR, heads)
     for load in loads:
-        load.start()
-    for n in range(map_ref.shape[0]):
-        map_ref[n] = -1
-    for load in loads[2:]:
         load.wait()
-
-    def entry(j, carry):
-        dest = dest_ref[0, j]
-        base = dest * CAP
-        taken = jnp.where(map_ref[base] >= 0, 1, 0)
-
-        @pl.when(dest != me)
-        def _():
-            map_ref[base + taken] = slot_ref[0, j]
-
-        return carry
-
-    lax.fori_loop(0, entries, entry, 0)
-    loads[1].wait()
-    loads[0].wait()
-    def store_of(n):
-        part = pl.ds(n * CAP, CAP)
-        return pltpu.make_async_copy(buf_ref.at[part], out_any.at[part], out_sem.at[n])
-
-    masks = make_masks(CAP, heads, 0)
-    gamma = gamma_row(table_ref, index_ref, CAP, heads)
-
-    def fill(n, carry):
-        slots, keys, values, keeps = [], [], [], []
-        for position in range(CAP):
-            found = map_ref[n * CAP + position]
-            slot = jnp.maximum(found, 0)
-            on = active_ref[slot] > 0
-            here = jnp.where(found >= 0, 1.0, 0.0)
-            tokens = tok_ref[slot].astype(jnp.float32)
-            slots.append(slot)
-            keys.append(tokens[1] * jnp.where(on, here, 0.0))
-            values.append(tokens[2])
-            keeps.append([here * jnp.where(on, decay(table_ref, index_ref, h) ** 2, 1.0) for h in range(heads)])
-        added = outer(*factors(keys, values, gamma, masks))
-        for position in range(CAP):
+    for pair in range(count // PAIR):
+        slots = [pair * PAIR + n for n in range(PAIR)]
+        tokens = [tok_ref[slot].astype(jnp.float32) for slot in slots]
+        on = [active_ref[slot] > 0 for slot in slots]
+        keys = [token[1] * jnp.where(flag, 1.0, 0.0) for token, flag in zip(tokens, on)]
+        added = outer(*factors(keys, [token[2] for token in tokens], gammas, masks))
+        for n, slot in enumerate(slots):
             for h in range(heads):
-                at = (position * heads + h) * W
-                final = keeps[position][h] * state_ref[slots[position], h] + added[at : at + W]
-                buf_ref[n * CAP + position, h] = final.astype(jnp.bfloat16)
-        store_of(n).start()
-        return carry
-
-    lax.fori_loop(0, groups, fill, 0, unroll=groups)
-    for n in range(groups):
-        store_of(n).wait()
+                keep = jnp.where(on[n], decay(table_ref, index_ref, h) ** 2, 1.0)
+                top = (n * heads + h) * W
+                final = keep * state_ref[slot, h] + added[top : top + W]
+                buf_ref[slot, h] = final.astype(jnp.bfloat16)
+    for n in range(spare):
+
+        @pl.when(row_ref[n] < count)
+        def _(n=n):
+            store_of(n, row_ref[n]).start()
+
+    for n in range(spare):
+        store_of(n, 0).wait()
 
 
 def decode_kernel(
@@ -374,10 +372,11 @@
             *scalar_scratch,
             pltpu.VMEM(tokens.shape, bf16),
             pltpu.VMEM(state.shape, f32),
-            pltpu.VMEM(moved, bf16),
-            pltpu.SMEM((groups * CAP,), jnp.int32),
-            dma((7,)),
-            dma((groups,)),
+            pltpu.VMEM((count + 1,) + pair[1:], bf16),
+            pltpu.SMEM((moved[0] + 1,), jnp.int32),
+            dma((6,)),
+            dma((count // PAIR,)),
+            dma((moved[0],)),
         ],
         compiler_params=params(),
         cost_estimate=pl.CostEstimate(flops=32 * 20 * width * width, bytes_accessed=8 << 20, transcendentals=0),

time: 65.3 us -> 65.2 us (level)
  no operation moved by 1% of the time
where the time goes in v4:
time: 65.2 us; the launch traced here: 65 us
  starting transfers between devices  27.5 us (42%)
  waiting for transfers between devices  26 us (40%)
  Pallas kernels  10.8 us (17%)
  between operations  0.68 us (1%)
    ppermute x6, waiting for transfers between devices, shift_x(): lax.ppermute(value, 'tensor', [(x * SIDE + y, (x + d) % SIDE * SIDE + y)...  12.8 us
    all_to_all x1, starting transfers between devices, body(): lax.all_to_all(leaving, 'batch', split_axis=0, concat_axis=0, tiled=True)  9.95 us
    ppermute x6, starting transfers between devices, shift_x(): lax.ppermute(value, 'tensor', [(x * SIDE + y, (x + d) % SIDE * SIDE + y)...  9.37 us
    ppermute x6, starting transfers between devices, shift_y(): lax.ppermute(value, 'tensor', [(x * SIDE + y, x * SIDE + (y + d) % SIDE)...  8.16 us
    all_to_all x1, waiting for transfers between devices, body(): lax.all_to_all(leaving, 'batch', split_axis=0, concat_axis=0, tiled=True)  7.04 us
    ppermute x6, waiting for transfers between devices, shift_y(): lax.ppermute(value, 'tensor', [(x * SIDE + y, x * SIDE + (y + d) % SIDE)...  6.09 us
    pallas_call x1, Pallas kernels, body(): pl.pallas_call(decode_kernel, out_shape=(pltpu.HBM(state.shape, f32), jax...  4.5 us
    pallas_call x1, Pallas kernels, body(): pl.pallas_call(leave_kernel, out_shape=pltpu.HBM(moved, bf16), in_specs=[...  3.35 us
  transfers between devices with their start and end apart: 13, of which 10 were waited for; matrix products, arithmetic and copies ran while one was open for 0% of the time, Pallas kernels for 8%

profile of v4, /device:TPU:1, one launch (start us, length us, event | category | flops | bytes accessed | tf_op | source)
XLA Modules:
  0.0 65.0 jit_solution(4340324920768750056)
XLA Ops:
  0.6 3.3 %leave.1.after_any = bf16[32,2,128,128]{3,2,1,0:T(8,128)(2,1)} custom-call(f32[16]{0:T(128)} %table_any.3, s32[2]{0:T(128)} %index_any.3, s32[16]{0:T(128)} %active_any.3, s32[1,16]{1,0:T(1,128)} %slot_any.3, s32[1,16]{1,0:T(1,128)} %dest_any.3, bf16[16,3,2,256]{3,2,1,0:T(2,128)(2,1)} %bitcast.1, f32[16,2,128,128]{3,2,1,0:T(8,128)} %state_any.3), custom_call_target="tpu_custom_call" | custom-call | flops 10485760 | bytes 8388608 | tf_op jit(solution)/shard_map/leave/pallas_call | solution.py:366
  4.0 10.0 %all-to-all-start = ((bf16[32,2,128,128]{3,2,1,0:T(8,128)(2,1)}), bf16[32,2,128,128]{3,2,1,0:T(8,128)(2,1)S(1)}, u32[]{:S(2)}, u32[]{:S(2)}) async-start(bf16[32,2,128,128]{3,2,1,0:T(8,128)(2,1)} %leave.1.after_any), calls=%async_computation | async-start | bytes 4194304 | tf_op jit(solution)/shard_map/all_to_all | solution.py:385
  14.0 4.5 %decode.1 = (f32[16,2,128,128]{3,2,1,0:T(8,128)}, f32[4,32,512]{2,1,0:T(8,128)S(1)}, f32[4,32,512]{2,1,0:T(8,128)}, f32[4,32,512]{2,1,0:T(8,128)}, f32[4,32,512]{2,1,0:T(8,128)}) custom-call(f32[16]{0:T(128)} %table_any.3, s32[2]{0:T(128)} %index_any.3, s32[16]{0:T(128)} %active_any.3, s32[1,16]{1,0:T(1,128)} %slot_any.3, s32[1,16]{1,0:T(1,128)} %dest_any.3, ...), custom_call_target="tpu_custom_call" | custom-call | flops 10485760 | bytes 8388608 | tf_op jit(solution)/shard_map/decode/pallas_call | solution.py:387
  18.5 1.3 %collective-permute-start = (f32[4,32,512]{2,1,0:T(8,128)}, f32[4,32,512]{2,1,0:T(8,128)S(1)}, u32[]{:S(2)}, u32[]{:S(2)}) collective-permute-start(f32[4,32,512]{2,1,0:T(8,128)} %get-tuple-element.18), channel_id=1, source_target_pairs={{0,4},{1,5},{2,6},{3,7},{4,8},{5,9},{6,10},{7,11},{8,12},{9,13},{1... | collective-permute-start | bytes 786440 | tf_op jit(solution)/shard_map/ppermute | solution.py:317
  19.8 2.4 %collective-permute-start.1 = (f32[4,32,512]{2,1,0:T(8,128)}, f32[4,32,512]{2,1,0:T(8,128)S(1)}, u32[]{:S(2)}, u32[]{:S(2)}) collective-permute-start(f32[4,32,512]{2,1,0:T(8,128)} %get-tuple-element.19), channel_id=1, source_target_pairs={{0,8},{1,9},{2,10},{3,11},{4,12},{5,13},{6,14},{7,15},{8,0},{9,1},... | collective-permute-start | bytes 786440 | tf_op jit(solution)/shard_map/ppermute | solution.py:317
  22.2 1.2 %collective-permute-start.2 = (f32[4,32,512]{2,1,0:T(8,128)}, f32[4,32,512]{2,1,0:T(8,128)S(1)}, u32[]{:S(2)}, u32[]{:S(2)}) collective-permute-start(f32[4,32,512]{2,1,0:T(8,128)} %get-tuple-element.20), channel_id=1, source_target_pairs={{0,12},{1,13},{2,14},{3,15},{4,0},{5,1},{6,2},{7,3},{8,4},{9,5},{1... | collective-permute-start | bytes 786440 | tf_op jit(solution)/shard_map/ppermute | solution.py:317
  23.4 4.5 %collective-permute-done.b_ref = f32[4,32,512]{2,1,0:T(8,128)S(1)} collective-permute-done((f32[4,32,512]{2,1,0:T(8,128)}, f32[4,32,512]{2,1,0:T(8,128)S(1)}, u32[]{:S(2)}, u32[]{:S(2)}) %collective-permute-start) | collective-permute-done | bytes 262176 | tf_op jit(solution)/shard_map/ppermute | solution.py:317
  27.8 6.6 %collective-permute-done.1.c_ref = f32[4,32,512]{2,1,0:T(8,128)S(1)} collective-permute-done((f32[4,32,512]{2,1,0:T(8,128)}, f32[4,32,512]{2,1,0:T(8,128)S(1)}, u32[]{:S(2)}, u32[]{:S(2)}) %collective-permute-start.1) | collective-permute-done | bytes 262176 | tf_op jit(solution)/shard_map/ppermute | solution.py:317
  34.5 1.4 %collective-permute-start.3 = (f32[32,512]{1,0:T(8,128)S(1)}, f32[32,512]{1,0:T(8,128)S(1)}, u32[]{:S(2)}, u32[]{:S(2)}) collective-permute-start(f32[32,512]{1,0:T(8,128)S(1)} %get-tuple-element.22), channel_id=1, source_target_pairs={{0,1},{1,2},{2,3},{3,0},{4,5},{5,6},{6,7},{7,4},{8,9},{9,10},{10,1... | collective-permute-start | bytes 196616 | tf_op jit(solution)/shard_map/ppermute | solution.py:323
  35.9 2.6 %collective-permute-start.4 = (f32[32,512]{1,0:T(8,128)S(1)}, f32[32,512]{1,0:T(8,128)S(1)}, u32[]{:S(2)}, u32[]{:S(2)}) collective-permute-start(f32[32,512]{1,0:T(8,128)S(1)} %get-tuple-element.23), channel_id=1, source_target_pairs={{0,2},{1,3},{2,0},{3,1},{4,6},{5,7},{6,4},{7,5},{8,10},{9,11},{10,... | collective-permute-start | bytes 196616 | tf_op jit(solution)/shard_map/ppermute | solution.py:323
  38.5 1.1 %collective-permute-start.5 = (f32[32,512]{1,0:T(8,128)S(1)}, f32[32,512]{1,0:T(8,128)S(1)}, u32[]{:S(2)}, u32[]{:S(2)}) collective-permute-start(f32[32,512]{1,0:T(8,128)S(1)} %get-tuple-element.24), channel_id=1, source_target_pairs={{0,3},{1,0},{2,1},{3,2},{4,7},{5,4},{6,5},{7,6},{8,11},{9,8},{10,9... | collective-permute-start | bytes 196616 | tf_op jit(solution)/shard_map/ppermute | solution.py:323
  39.6 1.6 %collective-permute-done.4.c_ref = f32[32,512]{1,0:T(8,128)S(1)} collective-permute-done((f32[32,512]{1,0:T(8,128)S(1)}, f32[32,512]{1,0:T(8,128)S(1)}, u32[]{:S(2)}, u32[]{:S(2)}) %collective-permute-start.4) | collective-permute-done | bytes 65568 | tf_op jit(solution)/shard_map/ppermute | solution.py:323
  41.2 0.9 %collective-permute-done.5.d_ref = f32[32,512]{1,0:T(8,128)S(1)} collective-permute-done((f32[32,512]{1,0:T(8,128)S(1)}, f32[32,512]{1,0:T(8,128)S(1)}, u32[]{:S(2)}, u32[]{:S(2)}) %collective-permute-start.5) | collective-permute-done | bytes 65568 | tf_op jit(solution)/shard_map/ppermute | solution.py:323
  42.2 1.1 %collective-permute-start.6 = (f32[32,128]{1,0:T(8,128)S(1)}, f32[32,128]{1,0:T(8,128)S(1)}, u32[]{:S(2)}, u32[]{:S(2)}) collective-permute-start(f32[32,128]{1,0:T(8,128)S(1)} %get-tuple-element.26), channel_id=1, source_target_pairs={{0,4},{1,5},{2,6},{3,7},{4,8},{5,9},{6,10},{7,11},{8,12},{9,13},{1... | collective-permute-start | bytes 49160 | tf_op jit(solution)/shard_map/ppermute | solution.py:317
  43.3 2.3 %collective-permute-start.7 = (f32[32,128]{1,0:T(8,128)S(1)}, f32[32,128]{1,0:T(8,128)S(1)}, u32[]{:S(2)}, u32[]{:S(2)}) collective-permute-start(f32[32,128]{1,0:T(8,128)S(1)} %get-tuple-element.26), channel_id=1, source_target_pairs={{0,8},{1,9},{2,10},{3,11},{4,12},{5,13},{6,14},{7,15},{8,0},{9,1},... | collective-permute-start | bytes 49160 | tf_op jit(solution)/shard_map/ppermute | solution.py:317
  45.6 1.1 %collective-permute-start.8 = (f32[32,128]{1,0:T(8,128)S(1)}, f32[32,128]{1,0:T(8,128)S(1)}, u32[]{:S(2)}, u32[]{:S(2)}) collective-permute-start(f32[32,128]{1,0:T(8,128)S(1)} %get-tuple-element.26), channel_id=1, source_target_pairs={{0,12},{1,13},{2,14},{3,15},{4,0},{5,1},{6,2},{7,3},{8,4},{9,5},{1... | collective-permute-start | bytes 49160 | tf_op jit(solution)/shard_map/ppermute | solution.py:317
  46.7 1.0 %collective-permute-done.7 = f32[32,128]{1,0:T(8,128)S(1)} collective-permute-done((f32[32,128]{1,0:T(8,128)S(1)}, f32[32,128]{1,0:T(8,128)S(1)}, u32[]{:S(2)}, u32[]{:S(2)}) %collective-permute-start.7) | collective-permute-done | bytes 16416 | tf_op jit(solution)/shard_map/ppermute | solution.py:317
  47.7 0.8 %collective-permute-done.8 = f32[32,128]{1,0:T(8,128)S(1)} collective-permute-done((f32[32,128]{1,0:T(8,128)S(1)}, f32[32,128]{1,0:T(8,128)S(1)}, u32[]{:S(2)}, u32[]{:S(2)}) %collective-permute-start.8) | collective-permute-done | bytes 16416 | tf_op jit(solution)/shard_map/ppermute | solution.py:317
  48.5 1.6 %collective-permute-start.10 = (f32[32,128]{1,0:T(8,128)S(1)}, f32[32,128]{1,0:T(8,128)S(1)}, u32[]{:S(2)}, u32[]{:S(2)}) collective-permute-start(f32[32,128]{1,0:T(8,128)S(1)} %add_add_fusion.a_ref), channel_id=1, source_target_pairs={{0,2},{1,3},{2,0},{3,1},{4,6},{5,7},{6,4},{7,5},{8,10},{9,11},{10,... | collective-permute-start | bytes 49160 | tf_op jit(solution)/shard_map/ppermute | solution.py:323
  50.1 1.0 %collective-permute-start.11 = (f32[32,128]{1,0:T(8,128)S(1)}, f32[32,128]{1,0:T(8,128)S(1)}, u32[]{:S(2)}, u32[]{:S(2)}) collective-permute-start(f32[32,128]{1,0:T(8,128)S(1)} %add_add_fusion.a_ref), channel_id=1, source_target_pairs={{0,3},{1,0},{2,1},{3,2},{4,7},{5,4},{6,5},{7,6},{8,11},{9,8},{10,9... | collective-permute-start | bytes 49160 | tf_op jit(solution)/shard_map/ppermute | solution.py:323
  51.6 1.3 %collective-permute-done.10.c_ref = f32[32,128]{1,0:T(8,128)S(1)} collective-permute-done((f32[32,128]{1,0:T(8,128)S(1)}, f32[32,128]{1,0:T(8,128)S(1)}, u32[]{:S(2)}, u32[]{:S(2)}) %collective-permute-start.10) | collective-permute-done | bytes 16416 | tf_op jit(solution)/shard_map/ppermute | solution.py:323
  53.0 2.2 %collective-permute-done.9.b_ref = f32[32,128]{1,0:T(8,128)S(1)} collective-permute-done((f32[32,128]{1,0:T(8,128)S(1)}, f32[32,128]{1,0:T(8,128)S(1)}, u32[]{:S(2)}, u32[]{:S(2)}) %collective-permute-start.9) | collective-permute-done | bytes 16416 | tf_op jit(solution)/shard_map/ppermute | solution.py:323
  55.8 7.0 %all-to-all-done.landed_ref = bf16[32,2,128,128]{3,2,1,0:T(8,128)(2,1)S(1)} async-done(((bf16[32,2,128,128]{3,2,1,0:T(8,128)(2,1)}), bf16[32,2,128,128]{3,2,1,0:T(8,128)(2,1)S(1)}, u32[]{:S(2)}, u32[]{:S(2)}) %all-to-all-start) | async-done | bytes 2097184 | tf_op jit(solution)/shard_map/all_to_all | solution.py:385
  62.9 2.1 %widen.1 = f32[32,2,128,128]{3,2,1,0:T(8,128)} custom-call(bf16[32,2,128,128]{3,2,1,0:T(8,128)(2,1)S(1)} %all-to-all-done.landed_ref), custom_call_target="tpu_custom_call" | custom-call | tf_op jit(solution)/shard_map/widen/pallas_call | solution.py:445
  (14 shorter events, 1.5 us)
Async XLA Ops:
  4.0 58.9 %all-to-all-start = ((bf16[32,2,128,128]{3,2,1,0:T(8,128)(2,1)}), bf16[32,2,128,128]{3,2,1,0:T(8,128)(2,1)S(1)}, u32[]{:S(2)}, u32[]{:S(2)}) async-start(bf16[32,2,128,128]{3,2,1,0:T(8,128)(2,1)} %leave.1.after_any), calls=%async_computation | async-start | bytes 4194304 | tf_op jit(solution)/shard_map/all_to_all | solution.py:385
  13.9 28.2 %copy-start = (bf16[16,2,512]{2,1,0:T(2,128)(2,1)S(1)}, bf16[16,2,512]{2,1,0:T(2,128)(2,1)}, u32[]{:S(2)}) copy-start(bf16[16,2,512]{2,1,0:T(2,128)(2,1)} %residual_ref.1) | copy-start | bytes 98308
  13.9 37.6 %copy-start.1 = (bf16[512]{0:T(512)(128)(2,1)S(1)}, bf16[512]{0:T(512)(128)(2,1)}, u32[]{:S(2)}) copy-start(bf16[512]{0:T(512)(128)(2,1)} %param.18) | copy-start | bytes 3076
  18.5 9.4 %collective-permute-start = (f32[4,32,512]{2,1,0:T(8,128)}, f32[4,32,512]{2,1,0:T(8,128)S(1)}, u32[]{:S(2)}, u32[]{:S(2)}) collective-permute-start(f32[4,32,512]{2,1,0:T(8,128)} %get-tuple-element.18), channel_id=1, source_target_pairs={{0,4},{1,5},{2,6},{3,7},{4,8},{5,9},{6,10},{7,11},{8,12},{9,13},{1... | collective-permute-start | bytes 786440 | tf_op jit(solution)/shard_map/ppermute | solution.py:317
  19.8 14.7 %collective-permute-start.1 = (f32[4,32,512]{2,1,0:T(8,128)}, f32[4,32,512]{2,1,0:T(8,128)S(1)}, u32[]{:S(2)}, u32[]{:S(2)}) collective-permute-start(f32[4,32,512]{2,1,0:T(8,128)} %get-tuple-element.19), channel_id=1, source_target_pairs={{0,8},{1,9},{2,10},{3,11},{4,12},{5,13},{6,14},{7,15},{8,0},{9,1},... | collective-permute-start | bytes 786440 | tf_op jit(solution)/shard_map/ppermute | solution.py:317
  22.2 12.2 %collective-permute-start.2 = (f32[4,32,512]{2,1,0:T(8,128)}, f32[4,32,512]{2,1,0:T(8,128)S(1)}, u32[]{:S(2)}, u32[]{:S(2)}) collective-permute-start(f32[4,32,512]{2,1,0:T(8,128)} %get-tuple-element.20), channel_id=1, source_target_pairs={{0,12},{1,13},{2,14},{3,15},{4,0},{5,1},{6,2},{7,3},{8,4},{9,5},{1... | collective-permute-start | bytes 786440 | tf_op jit(solution)/shard_map/ppermute | solution.py:317
  34.5 5.1 %collective-permute-start.3 = (f32[32,512]{1,0:T(8,128)S(1)}, f32[32,512]{1,0:T(8,128)S(1)}, u32[]{:S(2)}, u32[]{:S(2)}) collective-permute-start(f32[32,512]{1,0:T(8,128)S(1)} %get-tuple-element.22), channel_id=1, source_target_pairs={{0,1},{1,2},{2,3},{3,0},{4,5},{5,6},{6,7},{7,4},{8,9},{9,10},{10,1... | collective-permute-start | bytes 196616 | tf_op jit(solution)/shard_map/ppermute | solution.py:323
  35.9 5.3 %collective-permute-start.4 = (f32[32,512]{1,0:T(8,128)S(1)}, f32[32,512]{1,0:T(8,128)S(1)}, u32[]{:S(2)}, u32[]{:S(2)}) collective-permute-start(f32[32,512]{1,0:T(8,128)S(1)} %get-tuple-element.23), channel_id=1, source_target_pairs={{0,2},{1,3},{2,0},{3,1},{4,6},{5,7},{6,4},{7,5},{8,10},{9,11},{10,... | collective-permute-start | bytes 196616 | tf_op jit(solution)/shard_map/ppermute | solution.py:323
  38.5 3.6 %collective-permute-start.5 = (f32[32,512]{1,0:T(8,128)S(1)}, f32[32,512]{1,0:T(8,128)S(1)}, u32[]{:S(2)}, u32[]{:S(2)}) collective-permute-start(f32[32,512]{1,0:T(8,128)S(1)} %get-tuple-element.24), channel_id=1, source_target_pairs={{0,3},{1,0},{2,1},{3,2},{4,7},{5,4},{6,5},{7,6},{8,11},{9,8},{10,9... | collective-permute-start | bytes 196616 | tf_op jit(solution)/shard_map/ppermute | solution.py:323
  42.2 4.5 %collective-permute-start.6 = (f32[32,128]{1,0:T(8,128)S(1)}, f32[32,128]{1,0:T(8,128)S(1)}, u32[]{:S(2)}, u32[]{:S(2)}) collective-permute-start(f32[32,128]{1,0:T(8,128)S(1)} %get-tuple-element.26), channel_id=1, source_target_pairs={{0,4},{1,5},{2,6},{3,7},{4,8},{5,9},{6,10},{7,11},{8,12},{9,13},{1... | collective-permute-start | bytes 49160 | tf_op jit(solution)/shard_map/ppermute | solution.py:317
  43.3 4.4 %collective-permute-start.7 = (f32[32,128]{1,0:T(8,128)S(1)}, f32[32,128]{1,0:T(8,128)S(1)}, u32[]{:S(2)}, u32[]{:S(2)}) collective-permute-start(f32[32,128]{1,0:T(8,128)S(1)} %get-tuple-element.26), channel_id=1, source_target_pairs={{0,8},{1,9},{2,10},{3,11},{4,12},{5,13},{6,14},{7,15},{8,0},{9,1},... | collective-permute-start | bytes 49160 | tf_op jit(solution)/shard_map/ppermute | solution.py:317
  45.6 2.9 %collective-permute-start.8 = (f32[32,128]{1,0:T(8,128)S(1)}, f32[32,128]{1,0:T(8,128)S(1)}, u32[]{:S(2)}, u32[]{:S(2)}) collective-permute-start(f32[32,128]{1,0:T(8,128)S(1)} %get-tuple-element.26), channel_id=1, source_target_pairs={{0,12},{1,13},{2,14},{3,15},{4,0},{5,1},{6,2},{7,3},{8,4},{9,5},{1... | collective-permute-start | bytes 49160 | tf_op jit(solution)/shard_map/ppermute | solution.py:317
  48.5 4.4 %collective-permute-start.10 = (f32[32,128]{1,0:T(8,128)S(1)}, f32[32,128]{1,0:T(8,128)S(1)}, u32[]{:S(2)}, u32[]{:S(2)}) collective-permute-start(f32[32,128]{1,0:T(8,128)S(1)} %add_add_fusion.a_ref), channel_id=1, source_target_pairs={{0,2},{1,3},{2,0},{3,1},{4,6},{5,7},{6,4},{7,5},{8,10},{9,11},{10,... | collective-permute-start | bytes 49160 | tf_op jit(solution)/shard_map/ppermute | solution.py:323
  50.1 2.9 %collective-permute-start.11 = (f32[32,128]{1,0:T(8,128)S(1)}, f32[32,128]{1,0:T(8,128)S(1)}, u32[]{:S(2)}, u32[]{:S(2)}) collective-permute-start(f32[32,128]{1,0:T(8,128)S(1)} %add_add_fusion.a_ref), channel_id=1, source_target_pairs={{0,3},{1,0},{2,1},{3,2},{4,7},{5,4},{6,5},{7,6},{8,11},{9,8},{10,9... | collective-permute-start | bytes 49160 | tf_op jit(solution)/shard_map/ppermute | solution.py:323
  51.0 4.1 %collective-permute-start.9 = (f32[32,128]{1,0:T(8,128)S(1)}, f32[32,128]{1,0:T(8,128)S(1)}, u32[]{:S(2)}, u32[]{:S(2)}) collective-permute-start(f32[32,128]{1,0:T(8,128)S(1)} %add_add_fusion.a_ref), channel_id=1, source_target_pairs={{0,1},{1,2},{2,3},{3,0},{4,5},{5,6},{6,7},{7,4},{8,9},{9,10},{10,1... | collective-permute-start | bytes 49160 | tf_op jit(solution)/shard_map/ppermute | solution.py:323
